TPU v7x, 32 devices: a whole 2x2x4 slice. The times are simulated.
32 devices in a mesh: freq: 4 (over y, x), shot: 8 (over z, core).
Axes of the slice: x: 2, y: 2, z: 4, core: 2. Of those that a mesh axis runs over, the one named last changes fastest.
Arguments:
- source_field: bfloat16 [8, 8, 2, 128, 4096], P('freq', 'shot'), may hold values from -6 to 6
- receiver_field: bfloat16 [8, 8, 2, 128, 4096], P('freq', 'shot'), may hold values from -6 to 6
- angular_freq: float32 [8], P('freq'), may hold values from 2 to 40
- x_correction: bfloat16 [8, 2, 128, 128], P('freq'), may hold values from -0.25 to 0.25
- y_correction: bfloat16 [8, 2, 128, 128], P('freq'), may hold values from -0.25 to 0.25
- velocity: float32 [8, 128, 4096], P('shot'), may hold values from -1.2 to 1.2
- slab_owner: int32 [2], replicated, may hold values from 0 to 7, as said below
- apertures: int32 [8, 2], P('shot'), may hold values from 0 to 31
- tile_order: int32 [32], replicated, may hold values from 0 to 31, each once
Outputs:
- source_out: bfloat16 [8, 8, 2, 128, 4096], P('freq', 'shot')
- receiver_out: bfloat16 [8, 8, 2, 128, 4096], P('freq', 'shot')
- image: float32 [32, 2, 16384], P('shot', None, 'freq')
Inputs may be any that keep to these rules, and one draw needn't show every extreme that they name: `slab_owner`: the 2 entries are all different. `tile_order`: a permutation of all tiles.
All inputs are finite; a program needn't handle non-finite values.
Results may differ from a plain program's by a relative error of at most 0.0094.
Values sent between devices are 32-bit elements; how exact they have to be, the bound alone decides.
A program may use at most 128 MiB of HBM per device.

v0:
```python
import jax
import jax.numpy as jnp
from jax import lax
from jax.sharding import PartitionSpec as P

DEPTH = 2
TILE_DEV = 4


def spread(shard, axis, root):
    mine = lax.axis_index(axis) == root
    return lax.psum(jnp.where(mine, shard, jnp.zeros_like(shard)), axis)


def lens(field, phase_angle, conj_sign):
    real_part = field[:, :, 0].astype(jnp.float32)
    imag_part = field[:, :, 1].astype(jnp.float32)
    cosine = jnp.cos(phase_angle)
    sine = conj_sign * jnp.sin(phase_angle)
    new_real = real_part * cosine - imag_part * sine
    new_imag = real_part * sine + imag_part * cosine
    return jnp.stack([new_real, new_imag], axis=2).astype(jnp.bfloat16)


def sweep_x(field, correction, conj_sign):
    shape = field.shape
    width = correction.shape[-1]
    blocks = field.reshape(shape[:-1] + (shape[-1] // width, width))
    real_part = blocks[:, :, 0]
    imag_part = blocks[:, :, 1]
    c_real = correction[:, 0]
    c_imag = correction[:, 1]
    form = "fsynk,fkj->fsynj"
    new_real = (
        real_part.astype(jnp.float32)
        + jnp.einsum(form, real_part, c_real, preferred_element_type=jnp.float32)
        - conj_sign * jnp.einsum(form, imag_part, c_imag, preferred_element_type=jnp.float32)
    )
    new_imag = (
        imag_part.astype(jnp.float32)
        + jnp.einsum(form, imag_part, c_real, preferred_element_type=jnp.float32)
        + conj_sign * jnp.einsum(form, real_part, c_imag, preferred_element_type=jnp.float32)
    )
    return jnp.stack([new_real, new_imag], axis=2).reshape(shape).astype(jnp.bfloat16)


def sweep_y(field, correction, conj_sign):
    shape = field.shape
    width = correction.shape[-1]
    blocks = field.reshape(shape[:3] + (shape[3] // width, width, shape[4]))
    real_part = blocks[:, :, 0]
    imag_part = blocks[:, :, 1]
    c_real = correction[:, 0]
    c_imag = correction[:, 1]
    form = "fsnkx,fkj->fsnjx"
    new_real = (
        real_part.astype(jnp.float32)
        + jnp.einsum(form, real_part, c_real, preferred_element_type=jnp.float32)
        - conj_sign * jnp.einsum(form, imag_part, c_imag, preferred_element_type=jnp.float32)
    )
    new_imag = (
        imag_part.astype(jnp.float32)
        + jnp.einsum(form, imag_part, c_real, preferred_element_type=jnp.float32)
        + conj_sign * jnp.einsum(form, real_part, c_imag, preferred_element_type=jnp.float32)
    )
    return jnp.stack([new_real, new_imag], axis=2).reshape(shape).astype(jnp.bfloat16)


def fetch_slab(velocity, owner):
    return spread(velocity[0], "shot", owner)


def local(
    source_field,
    receiver_field,
    angular_freq,
    x_correction,
    y_correction,
    velocity,
    slab_owner,
    apertures,
    tile_order,
):
    shot_count = lax.axis_size("shot")
    freq_total = angular_freq.shape[0] * lax.axis_size("freq")
    tile_total = TILE_DEV * shot_count
    height = source_field.shape[3]
    width = source_field.shape[4]
    tile_width = width // tile_total
    tile_ids = apertures[0]
    collected = []
    for depth_step in range(DEPTH):
        velocity_slab = fetch_slab(velocity, slab_owner[depth_step])
        phase_angle = angular_freq[:, None, None, None] * velocity_slab[None, None]
        source_field = sweep_y(
            sweep_x(lens(source_field, phase_angle, 1.0), x_correction, 1.0), y_correction, 1.0
        )
        receiver_field = sweep_y(
            sweep_x(lens(receiver_field, phase_angle, -1.0), x_correction, -1.0), y_correction, -1.0
        )
        product_sum = source_field[:, 0, 0].astype(jnp.float32) * receiver_field[:, 0, 0].astype(
            jnp.float32
        ) + source_field[:, 0, 1].astype(jnp.float32) * receiver_field[:, 0, 1].astype(jnp.float32)
        image_term = jnp.sum(product_sum, axis=0) / freq_total
        blocks = image_term.reshape(height, tile_total, tile_width)
        picked = jnp.take(blocks, tile_ids, axis=1)
        collected.append(jnp.transpose(picked, (1, 0, 2)))
    stacked = jnp.stack(collected, axis=1)
    tile_parts = lax.psum_scatter(stacked, "freq", scatter_dimension=2, tiled=True)
    flat_parts = tile_parts.reshape(tile_parts.shape[0], tile_parts.shape[1], -1)
    match_table = (tile_order[:, None] == tile_ids[None, :]).astype(jnp.float32)
    dense_image = jnp.einsum(
        "pa,adl->pdl", match_table, flat_parts, precision=lax.Precision.HIGHEST
    )
    image = lax.psum_scatter(dense_image, "shot", scatter_dimension=0, tiled=True)
    return (source_field, receiver_field, image)


def solution(mesh):
    in_specs = (
        P("freq", "shot", None, None, None),
        P("freq", "shot", None, None, None),
        P("freq"),
        P("freq", None, None, None),
        P("freq", None, None, None),
        P("shot", None, None),
        P(),
        P("shot", None),
        P(),
    )
    out_specs = (
        P("freq", "shot", None, None, None),
        P("freq", "shot", None, None, None),
        P("shot", None, "freq"),
    )
    return jax.shard_map(local, mesh=mesh, in_specs=in_specs, out_specs=out_specs, check_vma=False)
```

profile of v0, /device:TPU:1, one launch (start us, length us, event | category | flops | bytes accessed | tf_op | source)
XLA Modules:
  0.0 300.0 jit_solution(2329481870537236375)
XLA Ops:
  7.2 1.3 fusion.143
  9.8 4.1 %select_bitcast_fusion.1 = (f32[128,4096]{1,0:T(8,128)}, f32[128,4096]{1,0:T(8,128)}) fusion(f32[1,128,4096]{2,1,0:T(8,128)} %param.16, pred[]{:T(512)S(6)} %eq.21, pred[]{:T(512)S(6)} %eq.22), kind=kLoop, calls=%fused_computation.110 | loop fusion | flops 1048576 | bytes 6291458 | tf_op jit(solution)/shard_map/jit(_where)/select_n | solution.py:12
  14.0 4.0 %fusion.142 = (bf16[2,1,1,128,4096]{4,3,2,1,0:T(8,128)(2,1)S(1)}, bf16[2,1,1,128,4096]{4,3,2,1,0:T(8,128)(2,1)}) fusion(bf16[2,1,2,128,4096]{4,3,2,1,0:T(8,128)(2,1)} %param.11), kind=kLoop, calls=%fused_computation.198 | loop fusion | bytes 8388608 | tf_op jit(solution)/shard_map/slice | solution.py:17
  17.9 4.1 %copy.156 = bf16[2,1,1,128,4096]{3,4,0,2,1:T(8,128)(2,1)} copy(bf16[2,1,1,128,4096]{4,3,2,1,0:T(8,128)(2,1)} %get-tuple-element.32) | data formatting | bytes 4194304
  22.0 2.5 copy.157
  24.5 4.0 %fusion.141 = (bf16[2,1,1,128,4096]{4,3,2,1,0:T(8,128)(2,1)S(1)}, bf16[2,1,1,128,4096]{4,3,2,1,0:T(8,128)(2,1)}) fusion(bf16[2,1,2,128,4096]{4,3,2,1,0:T(8,128)(2,1)} %param.12), kind=kLoop, calls=%fused_computation.197 | loop fusion | bytes 8388608 | tf_op jit(solution)/shard_map/slice | solution.py:17
  28.4 4.1 %copy.162 = bf16[2,1,1,128,4096]{3,4,0,2,1:T(8,128)(2,1)} copy(bf16[2,1,1,128,4096]{4,3,2,1,0:T(8,128)(2,1)} %get-tuple-element.30) | data formatting | bytes 4194304
  32.6 2.4 copy.163
  35.0 78.0 %all-reduce.7.cloned.1.call-done = (f32[128,4096]{1,0:T(8,128)}, f32[128,4096]{1,0:T(8,128)}) async-done(((f32[128,4096]{1,0:T(8,128)}, f32[128,4096]{1,0:T(8,128)}), (f32[128,4096]{1,0:T(8,128)}, f32[128,4096]{1,0:T(8,128)})) %all-reduce.7.cloned.1.call-update) | async-done | bytes 4194320 | tf_op jit(solution)/shard_map/psum | solution.py:12
  113.0 3.0 %copy.105 = f32[128,4096]{0,1:T(8,128)} copy(f32[128,4096]{1,0:T(8,128)} %get-tuple-element.17) | data formatting | bytes 4194304 | tf_op jit(solution)/shard_map/psum | solution.py:12
  116.1 20.8 %fusion.47 = (bf16[2,1,1,128,4096]{3,4,0,2,1:T(8,128)(2,1)S(1)}, bf16[2,1,1,128,4096]{3,4,0,2,1:T(8,128)(2,1)S(1)}, bf16[2,1,1,128,4096]{3,4,0,2,1:T(8,128)(2,1)S(1)}, bf16[2,1,1,128,4096]{3,4,0,2,1:T(8,128)(2,1)S(1)}) fusion(bf16[2,1,1,128,4096]{3,4,0,2,1:T(8,128)(2,1)} %copy.163, bf16[2,1,1,128,4096]{3,4,0,2,1:T(8,128)(2,1)} %copy.162, ...), kind=kLoop, calls=%fused_computation.79 | loop fusion | flops 23068672 | bytes 18874376 | tf_op jit(solution)/shard_map/convert.23
  137.7 0.7 fusion.76
  138.4 1.0 subtract_convert_fusion.1
  139.4 1.0 add_convert_fusion.1
  142.5 2.0 fusion.40
  145.2 0.7 fusion.84
  146.0 0.8 subtract_convert_fusion.3
  147.5 0.8 add_convert_fusion.3
  149.0 2.0 fusion.45
  151.0 2.0 fusion.44
  153.1 2.9 copy.115
  155.9 2.1 maximum_bitcast_fusion.2
  159.2 1.2 copy-done.4
  160.4 19.1 %fusion.55 = (bf16[2,1,1,128,4096]{3,4,0,2,1:T(8,128)(2,1)S(1)}, bf16[2,1,1,128,4096]{3,4,0,2,1:T(8,128)(2,1)S(1)}, f32[128,4096]{0,1:T(8,128)S(1)}, bf16[2,1,1,...) fusion(f32[128,4096]{0,1:T(8,128)S(1)} %copy-done.4, f32[2]{0:T(128)S(1)} %copy-done.8, ...), kind=kLoop, calls=%fused_computation.87 | loop fusion | flops 26738688 | bytes 20971528 | tf_op jit(solution)/shard_map/convert.35
  179.5 0.7 fusion.74
  180.3 0.7 fusion.72
  181.0 1.0 subtract_convert_fusion
  182.7 1.0 add_convert_fusion
  185.1 0.7 fusion.38
  185.8 0.7 fusion.82
  186.6 0.7 fusion.80
  187.3 0.8 subtract_convert_fusion.2
  188.9 0.9 add_convert_fusion.2
  192.7 1.6 copy-done
  194.3 1.6 add_reduce_fusion
  196.3 1.5 broadcast_multiply_fusion
  197.7 2.9 copy.132
  200.6 1.5 broadcast_multiply_fusion.1
  202.1 1.9 copy.131
  204.1 2.2 gather_fusion.1
  207.7 23.8 %reduce-scatter.3.cloned.1.call-done = f32[2,2,32,128]{3,2,0,1:T(8,128)} async-done(((f32[2,2,128,128]{3,2,0,1:T(8,128)}), f32[2,2,32,128]{3,2,0,1:T(8,128)}) %reduce-scatter.3.cloned.1.call-update) | async-done | bytes 65552 | tf_op jit(solution)/shard_map/reduce_scatter | solution.py:109
  231.5 0.9 reshape.780
  232.4 1.7 fusion.136
  235.3 6.4 %copy.134 = bf16[2,1,2,128,4096]{4,3,2,1,0:T(8,128)(2,1)} copy(bf16[2,1,2,128,4096]{3,4,0,2,1:T(8,128)(2,1)} %copy-done) | data formatting | bytes 8388608
  241.7 6.4 %copy.133 = bf16[2,1,2,128,4096]{4,3,2,1,0:T(8,128)(2,1)} copy(bf16[2,1,2,128,4096]{3,4,0,2,1:T(8,128)(2,1)} %copy-done.1) | data formatting | bytes 8388608
  248.1 43.7 %all-reduce.5.cloned.1.call-done = f32[32,2,4096]{2,0,1:T(8,128)} async-done(((f32[32,2,4096]{2,0,1:T(8,128)}), f32[32,2,4096]{2,0,1:T(8,128)}) %all-reduce.5.cloned.1.call-update) | async-done | bytes 1048592
  291.8 1.0 constant_dynamic-slice_fusion
  292.7 0.8 copy.135
  (52 shorter events, 14.1 us)
Async XLA Ops:
  7.2 105.9 %all-reduce.7.cloned.1.call-start = ((), (), s32[]{:S(2)}) async-start(), calls=%async_computation.3 | async-start | bytes 8388608 | tf_op jit(solution)/shard_map/psum | solution.py:12
  13.9 217.5 %reduce-scatter.3.cloned.1.call-start = ((), (), s32[]{:S(2)}) async-start(), calls=%async_computation.1 | async-start | bytes 327680 | tf_op jit(solution)/shard_map/reduce_scatter | solution.py:109
  32.6 2.5 copy-start.9
  113.0 3.0 %copy-start.7 = (bf16[2,1,1,128,4096]{3,4,0,2,1:T(8,128)(2,1)S(1)}, bf16[2,1,1,128,4096]{3,4,0,2,1:T(8,128)(2,1)}, u32[]{:S(2)}) copy-start(bf16[2,1,1,128,4096]{3,4,0,2,1:T(8,128)(2,1)} %copy.156) | copy-start | bytes 6291460
  113.0 3.0 %copy-start.8 = (f32[2]{0:T(128)S(1)}, f32[2]{0:T(128)}, u32[]{:S(2)}) copy-start(f32[2]{0:T(128)} %param.13) | copy-start | bytes 28
  116.1 20.9 %copy-start.2 = (bf16[2,2,128,128]{3,2,1,0:T(8,128)(2,1)S(1)}, bf16[2,2,128,128]{3,2,1,0:T(8,128)(2,1)}, u32[]{:S(2)}) copy-start(bf16[2,2,128,128]{3,2,1,0:T(8,128)(2,1)} %param.14) | copy-start | bytes 393220
  139.4 1.0 copy-start.3
  155.9 2.2 copy-start.5
  155.9 2.9 copy-start.6
  158.8 1.6 copy-start.4
  192.3 2.0 copy-start
  194.3 2.0 copy-start.1
  202.1 30.3 %copy-start.10 = (s32[32]{0:T(128)S(1)}, s32[32]{0:T(128)}, u32[]{:S(2)}) copy-start(s32[32]{0:T(128)} %param.19) | copy-start | bytes 388
  204.0 30.1 %copy-start.11 = (u32[32]{0:T(128)S(1)}, u32[32]{0:T(128)}, u32[]{:S(2)}) copy-start(u32[32]{0:T(128)} %constant.34) | copy-start | bytes 388
  207.6 84.1 %all-reduce.5.cloned.1.call-start = ((), (), s32[]{:S(2)}) async-start(), calls=%async_computation.2 | async-start | bytes 2097152
Sparse Core Ops, SparseCore 0:
  14.1 98.9 all-reduce.6
  207.7 23.6 reduce-scatter.2
  234.2 57.4 all-reduce.4
where the time goes:
time: 303 us; the launch traced here: 300 us
  waiting for transfers between devices  146 us (48%)
  local copies, waits for them, and re-layouts  55.6 us (18%)
  other arithmetic  52.7 us (17%)
  matrix products  30 us (10%)
  between operations  16 us (5%)
    psum x1, waiting for transfers between devices, spread(): return lax.psum(jnp.where(mine, shard, jnp.zeros_like(shard)), axis)  78 us
    unnamed x4, waiting for transfers between devices  43.7 us
    another operation x2, other arithmetic  40 us
    unnamed x33, local copies, waits for them, and re-layouts  32.1 us
    reduce_scatter x1, waiting for transfers between devices, local(): lax.psum_scatter(stacked, 'freq', scatter_dimension=2, tiled=True)  23.8 us
    slice x2, local copies, waits for them, and re-layouts, lens(): imag_part = field[:, :, 1].astype(jnp.float32)  7.91 us
  transfers between devices with their start and end apart: 3, of which 3 were waited for; matrix products, arithmetic and copies ran while one was open for 11% of the time, Pallas kernels for 0%

commit v1 on v0

v1 whole, which is shorter than its diff:
```python
import functools
import math

import jax
import jax.numpy as jnp
from jax import lax
from jax.experimental import pallas as pl
from jax.experimental.pallas import tpu as pltpu
from jax.sharding import PartitionSpec as P

DEPTH = 2
TILE_DEV = 4
CHUNK = 512
SIN = (4.44288292, -7.3082457, 3.60635441, -0.84611287, 0.10982695)
COS = (1.4142135, -6.97885099, 5.73946116, -1.88356292, 0.31069804)
F32 = jnp.float32
BF16 = jnp.bfloat16


def spread(shard, axis, root):
    mine = lax.axis_index(axis) == root
    return lax.psum(jnp.where(mine, shard, jnp.zeros_like(shard)), axis)


def horner(coefficients, z):
    total = jnp.full_like(z, coefficients[-1])
    for coefficient in coefficients[-2::-1]:
        total = total * z + coefficient
    return total


def cos_sin(turns):
    r = turns - jnp.round(turns)
    z = r * r
    half_sin = r * horner(SIN, z)
    half_cos = horner(COS, z)
    return 1.0 - half_sin * half_sin, half_sin * half_cos


def build_matrices(x_ref, y_ref, mx, my):
    for f in range(x_ref.shape[0]):
        xr, xi = x_ref[f, 0], x_ref[f, 1]
        yr = y_ref[f, 0].astype(F32).T.astype(BF16)
        yi = y_ref[f, 1].astype(F32).T.astype(BF16)
        for field in range(2):
            px, nx = (xi, -xi) if field == 0 else (-xi, xi)
            py, ny = (yi, -yi) if field == 0 else (-yi, yi)
            mx[f, field] = jnp.concatenate(
                [jnp.concatenate([xr, px], axis=1), jnp.concatenate([nx, xr], axis=1)], axis=0
            )
            my[f, field] = jnp.concatenate(
                [jnp.concatenate([yr, ny], axis=1), jnp.concatenate([py, yr], axis=1)], axis=0
            )


def step_field(re, im, cosine, sine, mx, my):
    height, width = re.shape
    re = re.astype(F32)
    im = im.astype(F32)
    lre = (re * cosine - im * sine).astype(BF16)
    lim = (re * sine + im * cosine).astype(BF16)
    tiles = width // 128
    rows = jnp.concatenate(
        [
            jnp.concatenate([lre[:, t * 128 : (t + 1) * 128], lim[:, t * 128 : (t + 1) * 128]], axis=1)
            for t in range(tiles)
        ],
        axis=0,
    )
    swept = (rows.astype(F32) + jnp.dot(rows, mx, preferred_element_type=F32)).astype(BF16)
    columns = jnp.concatenate(
        [
            jnp.concatenate([swept[t * height : (t + 1) * height, c : c + 128] for t in range(tiles)], axis=1)
            for c in (0, 128)
        ],
        axis=0,
    )
    out = (columns.astype(F32) + jnp.dot(my, columns, preferred_element_type=F32)).astype(BF16)
    return out[:height], out[height:]


def compute_kernel(
    freq_total, tiles_ref, freq_ref, source_ref, receiver_ref, x_ref, y_ref, slab_ref,
    source_out, receiver_out, term_ref, mx, my, kept,
):
    chunk = pl.program_id(0)

    @pl.when(chunk == 0)
    def _():
        build_matrices(x_ref, y_ref, mx, my)

    count = source_ref.shape[0]
    for f in range(count):
        scale = freq_ref[f] * (0.5 / math.pi)
        for d in range(DEPTH):
            cosine, sine = cos_sin(slab_ref[d] * scale)
            for field in range(2):
                first = (source_ref, receiver_ref)[field]
                if d == 0:
                    re, im = first[f, 0, 0], first[f, 0, 1]
                else:
                    re, im = kept[f, d - 1, field, 0], kept[f, d - 1, field, 1]
                re, im = step_field(
                    re, im, cosine, sine if field == 0 else -sine, mx[f, field], my[f, field]
                )
                kept[f, d, field, 0] = re
                kept[f, d, field, 1] = im
                if d == DEPTH - 1:
                    last = (source_out, receiver_out)[field]
                    last[f, 0, 0] = re
                    last[f, 0, 1] = im
    blocks = source_ref.shape[-1] // 128
    tile_width = term_ref.shape[-1]
    share = 128 // tile_width
    for a in range(term_ref.shape[0]):
        block = tiles_ref[a] // share - chunk * blocks
        place = tiles_ref[a] % share

        @pl.when(jnp.logical_and(block >= 0, block < blocks))
        def _():
            at = pl.ds(pl.multiple_of(block * 128, 128), 128)
            for d in range(DEPTH):
                total = jnp.zeros((term_ref.shape[2], 128), F32)
                for f in range(count):
                    for part in range(2):
                        total += kept[f, d, 0, part, :, at].astype(F32) * kept[f, d, 1, part, :, at].astype(F32)
                total = total * (1.0 / freq_total)
                picked = total[:, :tile_width]
                for p in range(1, share):
                    picked = jnp.where(place == p, total[:, p * tile_width : (p + 1) * tile_width], picked)
                term_ref[a, d] = picked


def compute(freq_total, tile_total, source, receiver, freq, xc, yc, slabs, tiles):
    count, _, _, height, width = source.shape
    tile_width = width // tile_total
    chunks = width // CHUNK
    field_spec = pl.BlockSpec((count, 1, 2, height, CHUNK), lambda i: (0, 0, 0, 0, i))
    smem = pl.BlockSpec(memory_space=pltpu.SMEM)
    whole = pl.BlockSpec(xc.shape, lambda i: (0, 0, 0, 0))
    aper = tiles.shape[0]
    return pl.pallas_call(
        functools.partial(compute_kernel, freq_total),
        grid=(chunks,),
        in_specs=[
            smem, smem, field_spec, field_spec, whole, whole,
            pl.BlockSpec((DEPTH, height, CHUNK), lambda i: (0, 0, i)),
        ],
        out_specs=[
            field_spec, field_spec,
            pl.BlockSpec((aper, DEPTH, height, tile_width), lambda i: (0, 0, 0, 0)),
        ],
        out_shape=[
            jax.ShapeDtypeStruct(source.shape, BF16),
            jax.ShapeDtypeStruct(receiver.shape, BF16),
            jax.ShapeDtypeStruct((aper, DEPTH, height, tile_width), F32),
        ],
        scratch_shapes=[
            pltpu.VMEM((count, 2, 256, 256), BF16),
            pltpu.VMEM((count, 2, 256, 256), BF16),
            pltpu.VMEM((count, DEPTH, 2, 2, height, CHUNK), BF16),
        ],
        compiler_params=pltpu.CompilerParams(vmem_limit_bytes=56 * 2**20),
        name="two_depth_steps",
    )(tiles, freq, source, receiver, xc, yc, slabs)


def local(
    source_field, receiver_field, angular_freq, x_correction, y_correction,
    velocity, slab_owner, apertures, tile_order,
):
    freq_total = angular_freq.shape[0] * lax.axis_size("freq")
    tile_ids = apertures[0]
    slabs = jnp.stack([spread(velocity[0], "shot", slab_owner[d]) for d in range(DEPTH)])
    source, receiver, terms = compute(
        freq_total, tile_order.shape[0], source_field, receiver_field, angular_freq, x_correction, y_correction, slabs, tile_ids
    )
    parts = lax.psum_scatter(terms, "freq", scatter_dimension=2, tiled=True)
    parts = parts.reshape(parts.shape[0], DEPTH, -1)
    every = lax.all_gather(parts, "shot", axis=0, tiled=True)
    ids = lax.all_gather(tile_ids, "shot", axis=0, tiled=True)
    mine = lax.dynamic_slice(tile_order, (lax.axis_index("shot") * TILE_DEV,), (TILE_DEV,))
    match = mine[:, None] == ids[None, :]
    image = jnp.sum(jnp.where(match[:, :, None, None], every[None], 0.0), axis=1)
    return source, receiver, image


def solution(mesh):
    in_specs = (
        P("freq", "shot", None, None, None),
        P("freq", "shot", None, None, None),
        P("freq"),
        P("freq", None, None, None),
        P("freq", None, None, None),
        P("shot", None, None),
        P(),
        P("shot", None),
        P(),
    )
    out_specs = (
        P("freq", "shot", None, None, None),
        P("freq", "shot", None, None, None),
        P("shot", None, "freq"),
    )
    return jax.shard_map(local, mesh=mesh, in_specs=in_specs, out_specs=out_specs, check_vma=False)
```

time: 303 us -> 190 us (0.63)
  local copies, waits for them, and re-layouts: 55.6 us -> 3.26 us
  other arithmetic: 52.7 us -> 9.87 us
  waiting for transfers between devices: 146 us -> 115 us
  matrix products: 30 us -> 0 us
  Pallas kernels: 0 us -> 23.5 us
  blocking collectives: 0 us -> 22.2 us
    unnamed x4 -> x2, waiting for transfers between devices: 43.7 us -> 0.03 us
    another operation x4 -> x1, other arithmetic: 40.8 us -> 4.61 us  [local(): jnp.stack([spread(velocity[0], 'shot', slab_owner[d]) for d in range(DEPT...]
    unnamed x33 -> x9, local copies, waits for them, and re-layouts: 32.1 us -> 0.68 us
    dot_general x33 -> x0, matrix products: 30 us -> none  [the longest x4 5.47 us: sweep_y(): jnp.einsum(form, real_part, c_imag, preferred_element_type=jnp.float32)]
    pallas_call x0 -> x1, Pallas kernels: none -> 23.5 us  [compute(): pl.pallas_call(functools.partial(compute_kernel, freq_total), grid=(chunk...]
    psum x1, waiting for transfers between devices: 78 us -> 99 us  [spread(): return lax.psum(jnp.where(mine, shard, jnp.zeros_like(shard)), axis)]
    all_gather x0 -> x1, blocking collectives: none -> 15.7 us  [local(): every = lax.all_gather(parts, 'shot', axis=0, tiled=True)]
    reduce_scatter x1, waiting for transfers between devices: 23.8 us -> 15.8 us  [local(): parts = lax.psum_scatter(terms, 'freq', scatter_dimension=2, tiled=True)]
  transfers between devices with their start and end apart: 3 -> 2, of which waited for: 3 -> 2; matrix products, arithmetic and copies ran while one was open for 11% -> 0% of each run, Pallas kernels for 0% -> 0%
where the time goes in v1:
time: 190 us
  waiting for transfers between devices  115 us (61%)
  Pallas kernels  23.5 us (12%)
  blocking collectives  22.2 us (12%)
  between operations  16 us (8%)
  other arithmetic  9.87 us (5%)
  local copies, waits for them, and re-layouts  3.26 us (2%)
    psum x1, waiting for transfers between devices, spread(): return lax.psum(jnp.where(mine, shard, jnp.zeros_like(shard)), axis)  99 us
    pallas_call x1, Pallas kernels, compute(): pl.pallas_call(functools.partial(compute_kernel, freq_total), grid=(chunk...  23.5 us
    reduce_scatter x1, waiting for transfers between devices, local(): parts = lax.psum_scatter(terms, 'freq', scatter_dimension=2, tiled=True)  15.8 us
    all_gather x1, blocking collectives, local(): every = lax.all_gather(parts, 'shot', axis=0, tiled=True)  15.7 us
    unnamed x1, blocking collectives  6.53 us
    another operation x1, other arithmetic, local(): jnp.stack([spread(velocity[0], 'shot', slab_owner[d]) for d in range(DEPT...  4.61 us
    select_n x1, other arithmetic, spread(): return lax.psum(jnp.where(mine, shard, jnp.zeros_like(shard)), axis)  4.08 us
  transfers between devices with their start and end apart: 2, of which 2 were waited for; matrix products, arithmetic and copies ran while one was open for 0% of the time, Pallas kernels for 0%

profile of v1, /device:TPU:1, one launch (start us, length us, event | category | flops | bytes accessed | tf_op | source)
XLA Modules:
  0.0 189.8 jit_solution(18272497927018046959)
XLA Ops:
  7.2 0.0 all-reduce.4.cloned.1.call-start
  7.2 1.3 fusion
  9.8 4.1 %broadcast_select_fusion.1 = (f32[1,128,4096]{2,1,0:T(8,128)}, f32[1,128,4096]{2,1,0:T(8,128)}) fusion(f32[1,128,4096]{2,1,0:T(8,128)} %param.14, pred[]{:T(512)S(6)} %eq.23, pred[]{:T(512)S(6)} %eq.24), kind=kLoop, calls=%fused_computation.3 | loop fusion | flops 1048576 | bytes 6291458 | tf_op jit(solution)/shard_map/jit(_where)/select_n | solution.py:22
  13.9 0.0 all-reduce.4.cloned.1.call-update
  13.9 0.0 reduce-scatter.2.cloned.1.call-start
  14.0 99.0 %all-reduce.4.cloned.1.call-done = (f32[1,128,4096]{2,1,0:T(8,128)}, f32[1,128,4096]{2,1,0:T(8,128)}) async-done(((f32[1,128,4096]{2,1,0:T(8,128)}, f32[1,128,4096]{2,1,0:T(8,128)}), (f32[1,128,4096]{2,1,0:T(8,128)}, f32[1,128,4096]{2,1,0:T(8,128)})) %all-reduce.4.cloned.1.call-update) | async-done | bytes 4194320 | tf_op jit(solution)/shard_map/psum | solution.py:22
  113.0 4.6 %pad_maximum_fusion.slab_ref = f32[2,128,4096]{2,1,0:T(8,128)} fusion(f32[1,128,4096]{2,1,0:T(8,128)} %get-tuple-element.9, f32[1,128,4096]{2,1,0:T(8,128)} %get-tuple-element.10), kind=kLoop, calls=%fused_computation | loop fusion | flops 1048576 | bytes 8388608 | tf_op jit(solution)/shard_map/stack | solution.py:174
  117.6 0.0 copy-start.2
  117.6 0.0 copy-start.1
  117.6 0.0 copy-start
  117.6 23.5 %two_depth_steps.1 = (bf16[2,1,2,128,4096]{4,3,2,1,0:T(8,128)(2,1)}, bf16[2,1,2,128,4096]{4,3,2,1,0:T(8,128)(2,1)}, f32[2,2,128,128]{3,2,1,0:T(8,128)}) custom-call(s32[2]{0:T(128)} %bitcast.7, f32[2]{0:T(128)} %freq_ref.1, bf16[2,1,2,128,4096]{4,3,2,1,0:T(8,128)(2,1)} %source_ref.1, bf16[2,1,2,128,4096]{4,3,2,1,0:T(8,128)(2,1)} %receiver_ref.1, ...), custom_call_target="tpu_custom_call" | custom-call | tf_op jit(solution)/shard_map/two_depth_steps/pallas_call | solution.py:142
  141.1 0.0 reduce-scatter.2.cloned.1.call-update
  141.1 0.0 copy-done.2
  141.2 0.6 dynamic-slice
  142.4 0.0 copy-done.1
  142.4 0.1 dynamic_slice.3
  142.5 0.0 copy-done
  142.5 0.1 bitcast_dynamic-update-slice_fusion
  142.6 6.5 %all-reduce = s32[16]{0:T(128)S(1)} all-reduce(s32[16]{0:T(128)S(1)} %bitcast_dynamic-update-slice_fusion), channel_id=2, replica_groups=mesh['freq'=4,'shot'=8] {'shot'}, use_global_device_ids=true, to_apply=%add | all-reduce | flops 16 | bytes 128
  149.1 0.1 broadcast_compare_fusion
  149.2 15.8 %reduce-scatter.2.cloned.1.call-done = f32[2,2,32,128]{3,2,1,0:T(8,128)} async-done(((f32[2,2,128,128]{3,2,1,0:T(8,128)}), f32[2,2,32,128]{3,2,1,0:T(8,128)}) %reduce-scatter.2.cloned.1.call-update) | async-done | bytes 65552 | tf_op jit(solution)/shard_map/reduce_scatter | solution.py:178
  165.0 0.9 reshape.43
  165.9 15.7 %all_gather.7 = f32[16,2,4096]{2,1,0:T(2,128)S(1)} all-gather(f32[2,2,4096]{2,1,0:T(2,128)S(1)} %reshape.43), channel_id=1, replica_groups=mesh['freq'=4,'shot'=8] {'shot'}, dimensions={0}, use_global_device_ids=true | all-gather | bytes 589824 | tf_op jit(solution)/shard_map/all_gather | solution.py:180
  181.6 0.3 copy.12
  181.9 1.1 select_reduce_fusion
  (1 shorter events, 0.0 us)
Async XLA Ops:
  7.2 105.9 %all-reduce.4.cloned.1.call-start = ((), (), s32[]{:S(2)}) async-start(), calls=%async_computation.2 | async-start | bytes 8388608 | tf_op jit(solution)/shard_map/psum | solution.py:22
  13.9 151.1 %reduce-scatter.2.cloned.1.call-start = ((), (), s32[]{:S(2)}) async-start(), calls=%async_computation.1 | async-start | bytes 327680 | tf_op jit(solution)/shard_map/reduce_scatter | solution.py:178
  117.6 23.5 %copy-start.2 = (u32[32]{0:T(128)S(1)}, u32[32]{0:T(128)}, u32[]{:S(2)}) copy-start(u32[32]{0:T(128)} %constant.22) | copy-start | bytes 388
  117.6 24.8 %copy-start.1 = (s32[32]{0:T(128)S(1)}, s32[32]{0:T(128)}, u32[]{:S(2)}) copy-start(s32[32]{0:T(128)} %param.17) | copy-start | bytes 388
  117.6 24.8 %copy-start = (s32[1,2]{1,0:T(1,128)S(1)}, s32[1,2]{1,0:T(1,128)}, u32[]{:S(2)}) copy-start(s32[1,2]{1,0:T(1,128)} %param.16) | copy-start | bytes 28
Sparse Core Ops, SparseCore 0:
  14.1 98.9 all-reduce.3
  141.3 23.6 reduce-scatter.1

commit v2 on v1

--- a/solution.py
+++ b/solution.py
@@ -15,11 +15,8 @@
 COS = (1.4142135, -6.97885099, 5.73946116, -1.88356292, 0.31069804)
 F32 = jnp.float32
 BF16 = jnp.bfloat16
-
-
-def spread(shard, axis, root):
-    mine = lax.axis_index(axis) == root
-    return lax.psum(jnp.where(mine, shard, jnp.zeros_like(shard)), axis)
+MESH = pl.DeviceIdType.MESH
+LAG = 2
 
 
 def horner(coefficients, z):
@@ -165,24 +162,327 @@
     )(tiles, freq, source, receiver, xc, yc, slabs)
 
 
+def greet(devices, count):
+    barrier = pltpu.get_barrier_semaphore()
+    for there, device in devices:
+        if there is None:
+            pl.semaphore_signal(barrier, inc=1, device_id=device, device_id_type=MESH)
+        else:
+
+            @pl.when(there)
+            def _(device=device):
+                pl.semaphore_signal(barrier, inc=1, device_id=device, device_id_type=MESH)
+
+    pl.semaphore_wait(barrier, count)
+
+
+def remote(src, dst, send, recv, device):
+    return pltpu.make_async_remote_copy(
+        src_ref=src, dst_ref=dst, send_sem=send, recv_sem=recv, device_id=device, device_id_type=MESH
+    )
+
+
+def slab_kernel(
+    freqs, shots, owner_ref, velocity_ref, out_ref,
+    slabs, sibling_part, mine, up_out, up_in, down_out, down_in,
+    pair_sem, up_sem, down_sem, plane_send, plane_recv, core_send, core_recv, out_sem,
+):
+    f = lax.axis_index("freq")
+    s = lax.axis_index("shot")
+    chain = shots // 2
+    z = s // 2
+    c = s % 2
+    rows, width = slabs.shape[2], slabs.shape[3]
+    chunks = width // CHUNK
+    sibling = (f, z * 2 + 1 - c)
+    above = (f, jnp.minimum(s + 2, shots - 2 + c))
+    below = (f, jnp.maximum(s - 2, c))
+    own = f * 2 + c
+    others = [(lax.rem(f + j, freqs), s) for j in range(1, freqs)]
+    has_below = z > 0
+    has_above = z < chain - 1
+    greet(
+        [(None, sibling)] + [(None, o) for o in others] + [(has_above, above), (has_below, below)],
+        freqs + has_above.astype(jnp.int32) + has_below.astype(jnp.int32),
+    )
+
+    def row_slice(index):
+        return pl.ds(pl.multiple_of(index * rows, 8), rows)
+
+    pair = remote(
+        velocity_ref.at[0, row_slice(f * 2 + 1 - c)], sibling_part, pair_sem.at[0], pair_sem.at[1], sibling
+    )
+    pair.start()
+
+    @pl.when(z == 0)
+    def _():
+        up_in[...] = jnp.zeros_like(up_in)
+
+    @pl.when(z == chain - 1)
+    def _():
+        down_in[...] = jnp.zeros_like(down_in)
+
+    pair.wait_recv()
+    own_part = velocity_ref[0, row_slice(own)]
+    other_part = sibling_part[...]
+    for d in range(DEPTH):
+        held = jnp.where(owner_ref[d] == s, own_part, jnp.zeros_like(own_part))
+        mine[d] = jnp.where(owner_ref[d] == z * 2 + 1 - c, other_part, held)
+
+    def at(k):
+        return pl.ds(pl.multiple_of(k * CHUNK, CHUNK), CHUNK)
+
+    def up_copy(k):
+        return remote(
+            up_out.at[:, :, at(k)], up_in.at[:, :, at(k)], up_sem.at[0, k], up_sem.at[1, k], above
+        )
+
+    def down_copy(k):
+        return remote(
+            down_out.at[:, :, at(k)], down_in.at[:, :, at(k)], down_sem.at[0, k], down_sem.at[1, k], below
+        )
+
+    def plane_copy(j, k):
+        place = slabs.at[:, own, :, at(k)]
+        return remote(place, place, plane_send.at[j - 1, k], plane_recv.at[j - 1, k], others[j - 1])
+
+    def core_copy(j, k):
+        place = slabs.at[:, lax.rem(f + freqs - j, freqs) * 2 + c, :, at(k)]
+        return remote(place, place, core_send.at[j, k], core_recv.at[j, k], sibling)
+
+    def arrived(j, k):
+        place = slabs.at[:, lax.rem(f + freqs - j, freqs) * 2 + c, :, at(k)]
+        return remote(place, place, plane_send.at[j - 1, k], plane_recv.at[j - 1, k], others[j - 1])
+
+    def core_arrived(j, k):
+        place = slabs.at[:, lax.rem(f + freqs - j, freqs) * 2 + 1 - c, :, at(k)]
+        return remote(place, place, core_send.at[j, k], core_recv.at[j, k], sibling)
+
+    def go_up(k):
+        @pl.when(has_below)
+        def _():
+            up_copy(k).wait_recv()
+
+        @pl.when(has_above)
+        def _():
+            up_out[:, :, at(k)] = up_in[:, :, at(k)] + mine[:, :, at(k)]
+            up_copy(k).start()
+
+    def go_down(k):
+        @pl.when(has_above)
+        def _():
+            down_copy(k).wait_recv()
+
+        @pl.when(has_below)
+        def _():
+            down_out[:, :, at(k)] = down_in[:, :, at(k)] + mine[:, :, at(k)]
+            down_copy(k).start()
+
+    lower = z < chain // 2
+    upper = z >= chain // 2
+
+    def out_copy(k):
+        return pltpu.make_async_copy(slabs.at[:, :, :, at(k)], out_ref.at[:, :, :, at(k)], out_sem.at[k])
+
+    def step(i, carry):
+        @pl.when(i < chunks)
+        def _():
+            @pl.when(lower)
+            def _():
+                go_up(i)
+
+            @pl.when(upper)
+            def _():
+                go_down(i)
+
+        @pl.when(jnp.logical_and(i >= LAG, i < chunks + LAG))
+        def _():
+            k = i - LAG
+
+            @pl.when(lower)
+            def _():
+                go_down(k)
+
+            @pl.when(upper)
+            def _():
+                go_up(k)
+
+            slabs[:, own, :, at(k)] = up_in[:, :, at(k)] + mine[:, :, at(k)] + down_in[:, :, at(k)]
+            for j in range(1, freqs):
+                plane_copy(j, k).start()
+            core_copy(0, k).start()
+
+        @pl.when(jnp.logical_and(i >= LAG + 1, i < chunks + LAG + 1))
+        def _():
+            k = i - LAG - 1
+            for j in range(1, freqs):
+                arrived(j, k).wait_recv()
+                core_copy(j, k).start()
+
+        @pl.when(i >= LAG + 2)
+        def _():
+            k = i - LAG - 2
+            for j in range(freqs):
+                core_arrived(j, k).wait_recv()
+            out_copy(k).start()
+
+        return carry
+
+    lax.fori_loop(0, chunks + LAG + 2, step, 0)
+    pair.wait_send()
+
+    def drain(k, carry):
+        @pl.when(has_above)
+        def _():
+            up_copy(k).wait_send()
+
+        @pl.when(has_below)
+        def _():
+            down_copy(k).wait_send()
+
+        for j in range(1, freqs):
+            plane_copy(j, k).wait_send()
+        for j in range(freqs):
+            core_copy(j, k).wait_send()
+        out_copy(k).wait()
+        return carry
+
+    lax.fori_loop(0, chunks, drain, 0)
+
+
+def exchange_slabs(freqs, shots, owners, velocity):
+    _, height, width = velocity.shape
+    rows = height // (2 * freqs)
+    chunks = width // CHUNK
+    strip = pltpu.VMEM((DEPTH, rows, width), F32)
+    dma = pltpu.SemaphoreType.DMA
+    slabs = pl.pallas_call(
+        functools.partial(slab_kernel, freqs, shots),
+        in_specs=[pl.BlockSpec(memory_space=pltpu.SMEM), pl.BlockSpec(memory_space=pltpu.VMEM)],
+        out_specs=pl.BlockSpec(memory_space=pl.ANY),
+        out_shape=jax.ShapeDtypeStruct((DEPTH, 2 * freqs, rows, width), F32),
+        scratch_shapes=[
+            pltpu.VMEM((DEPTH, 2 * freqs, rows, width), F32),
+            pltpu.VMEM((rows, width), F32),
+            strip, strip, strip, strip, strip,
+            dma((2,)), dma((2, chunks)), dma((2, chunks)),
+            dma((freqs - 1, chunks)), dma((freqs - 1, chunks)),
+            dma((freqs, chunks)), dma((freqs, chunks)), dma((chunks,)),
+        ],
+        compiler_params=pltpu.CompilerParams(
+            collective_id=0, has_side_effects=True, vmem_limit_bytes=48 * 2**20
+        ),
+        name="exchange_slabs",
+    )(owners, velocity)
+    return slabs.reshape(DEPTH, height, width)
+
+
+def image_kernel(
+    freqs, shots, ids_ref, order_ref, term_ref, out_ref,
+    landed, gathered, sum_send, sum_recv, shot_send, shot_recv, core_send, core_recv,
+):
+    f = lax.axis_index("freq")
+    s = lax.axis_index("shot")
+    chain = shots // 2
+    z = s // 2
+    c = s % 2
+    aper = term_ref.shape[0]
+    rows = out_ref.shape[2]
+    sibling = (f, z * 2 + 1 - c)
+    others = [(lax.rem(f + j, freqs), s) for j in range(1, freqs)]
+    chips = [lax.rem(z + j, chain) * 2 + c for j in range(chain)]
+    greet(
+        [(None, sibling)] + [(None, o) for o in others] + [(None, (f, chip)) for chip in chips[1:]],
+        freqs + chain - 1,
+    )
+
+    def row_slice(index):
+        return pl.ds(pl.multiple_of(index * rows, 8), rows)
+
+    sums = [
+        remote(
+            term_ref.at[:, :, row_slice(others[j - 1][0])], landed.at[j - 1],
+            sum_send.at[j - 1], sum_recv.at[j - 1], others[j - 1],
+        )
+        for j in range(1, freqs)
+    ]
+    for copy in sums:
+        copy.start()
+    for a in range(aper):
+        gathered[s, a, DEPTH * rows :] = jnp.full((8, term_ref.shape[3]), ids_ref[a].astype(F32))
+    total = term_ref[:, :, row_slice(f)]
+    for j in range(1, freqs):
+        sums[j - 1].wait_recv()
+        total = total + landed[j - 1]
+    gathered[s, :, : DEPTH * rows] = total.reshape(aper, DEPTH * rows, -1)
+
+    place = gathered.at[s]
+    sends = [
+        remote(place, place, shot_send.at[j - 1], shot_recv.at[j - 1], (f, chips[j])) for j in range(1, chain)
+    ]
+    for copy in sends:
+        copy.start()
+    forwards = []
+    for j in range(chain):
+        source = gathered.at[lax.rem(z + chain - j, chain) * 2 + c]
+        if j:
+            remote(source, source, shot_send.at[j - 1], shot_recv.at[j - 1], (f, chips[j])).wait_recv()
+        forwards.append(remote(source, source, core_send.at[j], core_recv.at[j], sibling))
+        forwards[-1].start()
+    for j in range(chain):
+        landing = gathered.at[lax.rem(z + chain - j, chain) * 2 + 1 - c]
+        remote(landing, landing, core_send.at[j], core_recv.at[j], sibling).wait_recv()
+
+    for p in range(TILE_DEV):
+        wanted = order_ref[s * TILE_DEV + p].astype(F32)
+        picked = jnp.zeros((DEPTH * rows // 8, 8, term_ref.shape[3]), F32)
+        for other in range(shots):
+            for a in range(aper):
+                hit = gathered[other, a, DEPTH * rows :] == wanted
+                value = gathered[other, a, : DEPTH * rows].reshape(picked.shape)
+                picked += jnp.where(hit[None], value, 0.0)
+        out_ref[p] = picked.reshape(DEPTH, rows, -1)
+    for copy in sums + sends + forwards:
+        copy.wait_send()
+
+
+def exchange_image(freqs, shots, ids, order, terms):
+    aper, _, height, tile_width = terms.shape
+    rows = height // freqs
+    chain = shots // 2
+    smem = pl.BlockSpec(memory_space=pltpu.SMEM)
+    vmem = pl.BlockSpec(memory_space=pltpu.VMEM)
+    dma = pltpu.SemaphoreType.DMA
+    image = pl.pallas_call(
+        functools.partial(image_kernel, freqs, shots),
+        in_specs=[smem, smem, vmem],
+        out_specs=vmem,
+        out_shape=jax.ShapeDtypeStruct((TILE_DEV, DEPTH, rows, tile_width), F32),
+        scratch_shapes=[
+            pltpu.VMEM((freqs - 1, aper, DEPTH, rows, tile_width), F32),
+            pltpu.VMEM((shots, aper, DEPTH * rows + 8, tile_width), F32),
+            dma((freqs - 1,)), dma((freqs - 1,)), dma((chain - 1,)), dma((chain - 1,)),
+            dma((chain,)), dma((chain,)),
+        ],
+        compiler_params=pltpu.CompilerParams(
+            collective_id=1, has_side_effects=True, vmem_limit_bytes=48 * 2**20
+        ),
+        name="exchange_image",
+    )(ids, order, terms)
+    return image.reshape(TILE_DEV, DEPTH, rows * tile_width)
+
+
 def local(
-    source_field, receiver_field, angular_freq, x_correction, y_correction,
+    freqs, shots, source_field, receiver_field, angular_freq, x_correction, y_correction,
     velocity, slab_owner, apertures, tile_order,
 ):
-    freq_total = angular_freq.shape[0] * lax.axis_size("freq")
     tile_ids = apertures[0]
-    slabs = jnp.stack([spread(velocity[0], "shot", slab_owner[d]) for d in range(DEPTH)])
+    slabs = exchange_slabs(freqs, shots, slab_owner, velocity)
     source, receiver, terms = compute(
-        freq_total, tile_order.shape[0], source_field, receiver_field, angular_freq, x_correction, y_correction, slabs, tile_ids
-    )
-    parts = lax.psum_scatter(terms, "freq", scatter_dimension=2, tiled=True)
-    parts = parts.reshape(parts.shape[0], DEPTH, -1)
-    every = lax.all_gather(parts, "shot", axis=0, tiled=True)
-    ids = lax.all_gather(tile_ids, "shot", axis=0, tiled=True)
-    mine = lax.dynamic_slice(tile_order, (lax.axis_index("shot") * TILE_DEV,), (TILE_DEV,))
-    match = mine[:, None] == ids[None, :]
-    image = jnp.sum(jnp.where(match[:, :, None, None], every[None], 0.0), axis=1)
-    return source, receiver, image
+        angular_freq.shape[0] * freqs, tile_order.shape[0],
+        source_field, receiver_field, angular_freq, x_correction, y_correction, slabs, tile_ids,
+    )
+    return source, receiver, exchange_image(freqs, shots, tile_ids, tile_order, terms)
 
 
 def solution(mesh):
@@ -202,4 +502,5 @@
         P("freq", "shot", None, None, None),
         P("shot", None, "freq"),
     )
-    return jax.shard_map(local, mesh=mesh, in_specs=in_specs, out_specs=out_specs, check_vma=False)
+    body = functools.partial(local, mesh.shape["freq"], mesh.shape["shot"])
+    return jax.shard_map(body, mesh=mesh, in_specs=in_specs, out_specs=out_specs, check_vma=False)

time: 190 us -> 108 us (0.57)
  waiting for transfers between devices: 115 us -> 0 us
  Pallas kernels: 23.5 us -> 104 us
  blocking collectives: 22.2 us -> 0 us
  between operations: 16 us -> 0.7 us
  other arithmetic: 9.87 us -> 0 us
    psum x1 -> x0, waiting for transfers between devices: 99 us -> none  [spread(): return lax.psum(jnp.where(mine, shard, jnp.zeros_like(shard)), axis)]
    pallas_call x0 -> x2, Pallas kernels: none -> 80.1 us  [the longest x1 64.1 us: exchange_slabs(): pl.pallas_call(functools.partial(slab_kernel, freqs, shots), in_specs=[pl...]
    reduce_scatter x1 -> x0, waiting for transfers between devices: 15.8 us -> none  [local(): parts = lax.psum_scatter(terms, 'freq', scatter_dimension=2, tiled=True)]
    all_gather x1 -> x0, blocking collectives: 15.7 us -> none  [local(): every = lax.all_gather(parts, 'shot', axis=0, tiled=True)]
    unnamed x1 -> x0, blocking collectives: 6.53 us -> none
    another operation x1 -> x0, other arithmetic: 4.61 us -> none  [local(): jnp.stack([spread(velocity[0], 'shot', slab_owner[d]) for d in range(DEPT...]
    select_n x1 -> x0, other arithmetic: 4.08 us -> none  [spread(): return lax.psum(jnp.where(mine, shard, jnp.zeros_like(shard)), axis)]
    unnamed x9 -> x10, local copies, waits for them, and re-layouts: 0.68 us -> 3.19 us
  transfers between devices with their start and end apart: 2 -> 0, of which waited for: 2 -> 0; matrix products, arithmetic and copies ran while one was open for 0% -> 0% of each run, Pallas kernels for 0% -> 0%
where the time goes in v2:
time: 108 us
  Pallas kernels  104 us (96%)
  local copies, waits for them, and re-layouts  3.92 us (4%)
    pallas_call x1, Pallas kernels, exchange_slabs(): pl.pallas_call(functools.partial(slab_kernel, freqs, shots), in_specs=[pl...  64.1 us
    pallas_call x1, Pallas kernels, compute(): pl.pallas_call(functools.partial(compute_kernel, freq_total), grid=(chunk...  23.5 us
    pallas_call x1, Pallas kernels, exchange_image(): pl.pallas_call(functools.partial(image_kernel, freqs, shots), in_specs=[s...  16 us
    unnamed x10, local copies, waits for them, and re-layouts  3.19 us

profile of v2, /device:TPU:1, one launch (start us, length us, event | category | flops | bytes accessed | tf_op | source)
XLA Modules:
  0.0 108.2 jit_solution(9228838722979723174)
XLA Ops:
  0.6 0.0 copy-start
  0.6 1.6 %copy-done = f32[1,128,4096]{2,1,0:T(8,128)S(1)} copy-done((f32[1,128,4096]{2,1,0:T(8,128)S(1)}, f32[1,128,4096]{2,1,0:T(8,128)}, u32[]{:S(2)}) %copy-start) | copy-done | bytes 2097176
  2.2 0.0 copy-start.3
  2.2 0.7 copy-done.3
  2.9 64.1 %exchange_slabs.1 = f32[2,8,16,4096]{3,2,1,0:T(8,128)} custom-call(s32[2]{0:T(128)S(1)} %copy-done.3, f32[1,128,4096]{2,1,0:T(8,128)S(1)} %copy-done), custom_call_target="tpu_custom_call" | custom-call | tf_op jit(solution)/shard_map/exchange_slabs/pallas_call | solution.py:359
  67.0 0.0 copy-start.2
  67.0 0.0 copy-start.4
  67.0 23.5 %two_depth_steps.1 = (bf16[2,1,2,128,4096]{4,3,2,1,0:T(8,128)(2,1)}, bf16[2,1,2,128,4096]{4,3,2,1,0:T(8,128)(2,1)}, f32[2,2,128,128]{3,2,1,0:T(8,128)}) custom-call(s32[2]{0:T(128)} %bitcast.4, f32[2]{0:T(128)} %freq_ref.1, bf16[2,1,2,128,4096]{4,3,2,1,0:T(8,128)(2,1)} %source_ref.1, bf16[2,1,2,128,4096]{4,3,2,1,0:T(8,128)(2,1)} %receiver_ref.1, ...), custom_call_target="tpu_custom_call" | custom-call | tf_op jit(solution)/shard_map/two_depth_steps/pallas_call | solution.py:139
  90.5 0.0 copy-done.2
  90.5 0.0 copy-done.4
  90.5 0.0 copy-start.1
  90.5 0.9 copy-done.1
  91.5 16.0 %exchange_image.1 = f32[4,2,32,128]{3,2,1,0:T(8,128)S(1)} custom-call(s32[2]{0:T(128)S(1)} %bitcast.5, s32[32]{0:T(128)S(1)} %copy-done.4, f32[2,2,128,128]{3,2,1,0:T(8,128)S(1)} %copy-done.1), custom_call_target="tpu_custom_call" | custom-call | tf_op jit(solution)/shard_map/exchange_image/pallas_call | solution.py:456
  107.5 0.7 reshape.13
Async XLA Ops:
  0.6 1.6 %copy-start = (f32[1,128,4096]{2,1,0:T(8,128)S(1)}, f32[1,128,4096]{2,1,0:T(8,128)}, u32[]{:S(2)}) copy-start(f32[1,128,4096]{2,1,0:T(8,128)} %velocity_ref.1) | copy-start | bytes 6291460
  2.2 0.7 copy-start.3
  67.0 23.5 %copy-start.2 = (s32[1,2]{1,0:T(1,128)S(1)}, s32[1,2]{1,0:T(1,128)}, u32[]{:S(2)}) copy-start(s32[1,2]{1,0:T(1,128)} %param.16) | copy-start | bytes 28
  67.0 23.5 %copy-start.4 = (s32[32]{0:T(128)S(1)}, s32[32]{0:T(128)}, u32[]{:S(2)}) copy-start(s32[32]{0:T(128)} %order_ref.1) | copy-start | bytes 388
  90.5 1.0 copy-start.1

commit v3 on v2

--- a/solution.py
+++ b/solution.py
@@ -10,13 +10,16 @@
 
 DEPTH = 2
 TILE_DEV = 4
-CHUNK = 512
+CHUNK = 256
+LAST_CHUNK = 512
 SIN = (4.44288292, -7.3082457, 3.60635441, -0.84611287, 0.10982695)
 COS = (1.4142135, -6.97885099, 5.73946116, -1.88356292, 0.31069804)
 F32 = jnp.float32
 BF16 = jnp.bfloat16
 MESH = pl.DeviceIdType.MESH
 LAG = 2
+PLANE_LAG = LAG + 3
+CORE_LAG = PLANE_LAG + 1
 
 
 def horner(coefficients, z):
@@ -34,93 +37,97 @@
     return 1.0 - half_sin * half_sin, half_sin * half_cos
 
 
-def build_matrices(x_ref, y_ref, mx, my):
-    for f in range(x_ref.shape[0]):
-        xr, xi = x_ref[f, 0], x_ref[f, 1]
-        yr = y_ref[f, 0].astype(F32).T.astype(BF16)
-        yi = y_ref[f, 1].astype(F32).T.astype(BF16)
-        for field in range(2):
-            px, nx = (xi, -xi) if field == 0 else (-xi, xi)
-            py, ny = (yi, -yi) if field == 0 else (-yi, yi)
-            mx[f, field] = jnp.concatenate(
-                [jnp.concatenate([xr, px], axis=1), jnp.concatenate([nx, xr], axis=1)], axis=0
-            )
-            my[f, field] = jnp.concatenate(
-                [jnp.concatenate([yr, ny], axis=1), jnp.concatenate([py, yr], axis=1)], axis=0
-            )
-
-
-def step_field(re, im, cosine, sine, mx, my):
-    height, width = re.shape
-    re = re.astype(F32)
-    im = im.astype(F32)
-    lre = (re * cosine - im * sine).astype(BF16)
-    lim = (re * sine + im * cosine).astype(BF16)
-    tiles = width // 128
+def pair_matrix(real, below_left, above_right):
+    return jnp.concatenate(
+        [jnp.concatenate([real, above_right], axis=1), jnp.concatenate([below_left, real], axis=1)], axis=0
+    )
+
+
+def x_matrix(x_ref, f):
+    return pair_matrix(x_ref[f, 0], -x_ref[f, 1], x_ref[f, 1])
+
+
+def y_matrix(y_ref, f):
+    real = y_ref[f, 0].astype(F32).T.astype(BF16)
+    imag = y_ref[f, 1].astype(F32).T.astype(BF16)
+    return pair_matrix(real, imag, -imag)
+
+
+def sweep_x(re, im, mx):
     rows = jnp.concatenate(
         [
-            jnp.concatenate([lre[:, t * 128 : (t + 1) * 128], lim[:, t * 128 : (t + 1) * 128]], axis=1)
-            for t in range(tiles)
+            jnp.concatenate([re[:, t : t + 128], im[:, t : t + 128]], axis=1)
+            for t in range(0, re.shape[1], 128)
         ],
         axis=0,
     )
     swept = (rows.astype(F32) + jnp.dot(rows, mx, preferred_element_type=F32)).astype(BF16)
-    columns = jnp.concatenate(
-        [
-            jnp.concatenate([swept[t * height : (t + 1) * height, c : c + 128] for t in range(tiles)], axis=1)
-            for c in (0, 128)
-        ],
-        axis=0,
-    )
-    out = (columns.astype(F32) + jnp.dot(my, columns, preferred_element_type=F32)).astype(BF16)
-    return out[:height], out[height:]
-
-
-def compute_kernel(
-    freq_total, tiles_ref, freq_ref, source_ref, receiver_ref, x_ref, y_ref, slab_ref,
-    source_out, receiver_out, term_ref, mx, my, kept,
+    height = re.shape[0]
+    return [
+        jnp.concatenate([swept[t : t + height, c : c + 128] for t in range(0, swept.shape[0], height)], axis=1)
+        for c in (0, 128)
+    ]
+
+
+def sweep_y(re, im, my):
+    columns = jnp.concatenate([re, im], axis=0)
+    out = columns.astype(F32) + jnp.dot(my, columns, preferred_element_type=F32)
+    return out[: re.shape[0]], out[re.shape[0] :]
+
+
+def last_kernel(
+    freq_total, ids_ref, y_ref, source_ref, receiver_ref, first_source, first_receiver, half_source, half_receiver,
+    source_out, receiver_out, term_ref, my, tiles, tile_sem,
 ):
-    chunk = pl.program_id(0)
-
-    @pl.when(chunk == 0)
-    def _():
-        build_matrices(x_ref, y_ref, mx, my)
-
-    count = source_ref.shape[0]
-    for f in range(count):
-        scale = freq_ref[f] * (0.5 / math.pi)
-        for d in range(DEPTH):
-            cosine, sine = cos_sin(slab_ref[d] * scale)
-            for field in range(2):
-                first = (source_ref, receiver_ref)[field]
-                if d == 0:
-                    re, im = first[f, 0, 0], first[f, 0, 1]
-                else:
-                    re, im = kept[f, d - 1, field, 0], kept[f, d - 1, field, 1]
-                re, im = step_field(
-                    re, im, cosine, sine if field == 0 else -sine, mx[f, field], my[f, field]
-                )
-                kept[f, d, field, 0] = re
-                kept[f, d, field, 1] = im
-                if d == DEPTH - 1:
-                    last = (source_out, receiver_out)[field]
-                    last[f, 0, 0] = re
-                    last[f, 0, 1] = im
-    blocks = source_ref.shape[-1] // 128
+    step = pl.program_id(0)
+    aper = term_ref.shape[0]
     tile_width = term_ref.shape[-1]
     share = 128 // tile_width
-    for a in range(term_ref.shape[0]):
-        block = tiles_ref[a] // share - chunk * blocks
-        place = tiles_ref[a] % share
-
-        @pl.when(jnp.logical_and(block >= 0, block < blocks))
-        def _():
-            at = pl.ds(pl.multiple_of(block * 128, 128), 128)
+    whole = ((first_source, first_receiver), (half_source, half_receiver))
+
+    def loads(a):
+        at = pl.ds(pl.multiple_of(ids_ref[a] // share * 128, 128), 128)
+        return [
+            pltpu.make_async_copy(
+                whole[d][field].at[:, 0, :, :, at], tiles.at[a, d, field], tile_sem.at[a, d, field]
+            )
+            for d in range(DEPTH)
+            for field in range(2)
+        ]
+
+    @pl.when(step == 0)
+    def _():
+        for a in range(aper):
+            for load in loads(a):
+                load.start()
+        for f in range(y_ref.shape[0]):
+            my[f] = y_matrix(y_ref, f)
+
+    for f in range(source_ref.shape[0]):
+        re, im = sweep_y(source_ref[f, 0, 0], source_ref[f, 0, 1], my[f])
+        source_out[f, 0, 0] = re.astype(BF16)
+        source_out[f, 0, 1] = im.astype(BF16)
+        re, im = sweep_y(receiver_ref[f, 0, 0], receiver_ref[f, 0, 1], my[f])
+        receiver_out[f, 0, 0] = re.astype(BF16)
+        receiver_out[f, 0, 1] = (-im).astype(BF16)
+
+    @pl.when(step == 1)
+    def _():
+        for a in range(aper):
+            for load in loads(a):
+                load.wait()
+            place = ids_ref[a] % share
             for d in range(DEPTH):
                 total = jnp.zeros((term_ref.shape[2], 128), F32)
-                for f in range(count):
-                    for part in range(2):
-                        total += kept[f, d, 0, part, :, at].astype(F32) * kept[f, d, 1, part, :, at].astype(F32)
+                for f in range(source_ref.shape[0]):
+                    re, im = [
+                        jnp.concatenate([tiles[a, d, field, f, part] for field in range(2)], axis=1)
+                        for part in range(2)
+                    ]
+                    if d == DEPTH - 1:
+                        re, im = [value.astype(BF16) for value in sweep_y(re, im, my[f])]
+                    re, im = re.astype(F32), im.astype(F32)
+                    total += re[:, :128] * re[:, 128:] - im[:, :128] * im[:, 128:]
                 total = total * (1.0 / freq_total)
                 picked = total[:, :tile_width]
                 for p in range(1, share):
@@ -128,38 +135,30 @@
                 term_ref[a, d] = picked
 
 
-def compute(freq_total, tile_total, source, receiver, freq, xc, yc, slabs, tiles):
+def last_sweep(freq_total, tile_total, ids, yc, first_source, first_receiver, source, receiver):
     count, _, _, height, width = source.shape
-    tile_width = width // tile_total
-    chunks = width // CHUNK
-    field_spec = pl.BlockSpec((count, 1, 2, height, CHUNK), lambda i: (0, 0, 0, 0, i))
-    smem = pl.BlockSpec(memory_space=pltpu.SMEM)
-    whole = pl.BlockSpec(xc.shape, lambda i: (0, 0, 0, 0))
-    aper = tiles.shape[0]
+    aper = ids.shape[0]
+    spec = pl.BlockSpec((count, 1, 2, height, LAST_CHUNK), lambda i: (0, 0, 0, 0, i))
+    shape = jax.ShapeDtypeStruct(source.shape, BF16)
+    term = (aper, DEPTH, height, width // tile_total)
+    anywhere = pl.BlockSpec(memory_space=pl.ANY)
     return pl.pallas_call(
-        functools.partial(compute_kernel, freq_total),
-        grid=(chunks,),
+        functools.partial(last_kernel, freq_total),
+        grid=(width // LAST_CHUNK,),
         in_specs=[
-            smem, smem, field_spec, field_spec, whole, whole,
-            pl.BlockSpec((DEPTH, height, CHUNK), lambda i: (0, 0, i)),
+            pl.BlockSpec(memory_space=pltpu.SMEM), pl.BlockSpec(yc.shape, lambda i: (0, 0, 0, 0)),
+            spec, spec, anywhere, anywhere, anywhere, anywhere,
         ],
-        out_specs=[
-            field_spec, field_spec,
-            pl.BlockSpec((aper, DEPTH, height, tile_width), lambda i: (0, 0, 0, 0)),
+        out_specs=[spec, spec, pl.BlockSpec(term, lambda i: (0, 0, 0, 0))],
+        out_shape=[shape, shape, jax.ShapeDtypeStruct(term, F32)],
+        scratch_shapes=[
+            pltpu.VMEM((count, 256, 256), BF16),
+            pltpu.VMEM((aper, DEPTH, 2, count, 2, height, 128), BF16),
+            pltpu.SemaphoreType.DMA((aper, DEPTH, 2)),
         ],
-        out_shape=[
-            jax.ShapeDtypeStruct(source.shape, BF16),
-            jax.ShapeDtypeStruct(receiver.shape, BF16),
-            jax.ShapeDtypeStruct((aper, DEPTH, height, tile_width), F32),
-        ],
-        scratch_shapes=[
-            pltpu.VMEM((count, 2, 256, 256), BF16),
-            pltpu.VMEM((count, 2, 256, 256), BF16),
-            pltpu.VMEM((count, DEPTH, 2, 2, height, CHUNK), BF16),
-        ],
-        compiler_params=pltpu.CompilerParams(vmem_limit_bytes=56 * 2**20),
-        name="two_depth_steps",
-    )(tiles, freq, source, receiver, xc, yc, slabs)
+        compiler_params=pltpu.CompilerParams(vmem_limit_bytes=48 * 2**20),
+        name="last_sweep",
+    )(ids, yc, source, receiver, first_source, first_receiver, source, receiver)
 
 
 def greet(devices, count):
@@ -183,9 +182,10 @@
 
 
 def slab_kernel(
-    freqs, shots, owner_ref, velocity_ref, out_ref,
-    slabs, sibling_part, mine, up_out, up_in, down_out, down_in,
-    pair_sem, up_sem, down_sem, plane_send, plane_recv, core_send, core_recv, out_sem,
+    freqs, shots, owner_ref, freq_ref, velocity_ref, source_ref, receiver_ref, x_ref, y_ref,
+    source_first, receiver_first, source_out, receiver_out,
+    slabs, own_part, sibling_part, mine, up_out, up_in, down_out, down_in, fields, stage, mx, my,
+    pair_sem, up_sem, down_sem, plane_send, plane_recv, core_send, core_recv, in_sem, out_sem,
 ):
     f = lax.axis_index("freq")
     s = lax.axis_index("shot")
@@ -198,6 +198,12 @@
     above = (f, jnp.minimum(s + 2, shots - 2 + c))
     below = (f, jnp.maximum(s - 2, c))
     own = f * 2 + c
+    field_refs = (source_ref, receiver_ref)
+    out_refs = (source_first, receiver_first, source_out, receiver_out)
+    count, height = source_ref.shape[0], source_ref.shape[3]
+    loads = [
+        pltpu.make_async_copy(field_refs[i].at[:, 0], fields.at[i], in_sem.at[i]) for i in range(2)
+    ]
     others = [(lax.rem(f + j, freqs), s) for j in range(1, freqs)]
     has_below = z > 0
     has_above = z < chain - 1
@@ -213,6 +219,13 @@
         velocity_ref.at[0, row_slice(f * 2 + 1 - c)], sibling_part, pair_sem.at[0], pair_sem.at[1], sibling
     )
     pair.start()
+    own_load = pltpu.make_async_copy(velocity_ref.at[0, row_slice(own)], own_part, in_sem.at[2])
+    own_load.start()
+    for load in loads:
+        load.start()
+    for i in range(count):
+        mx[i] = x_matrix(x_ref, i)
+        my[i] = y_matrix(y_ref, i)
 
     @pl.when(z == 0)
     def _():
@@ -222,12 +235,13 @@
     def _():
         down_in[...] = jnp.zeros_like(down_in)
 
+    own_load.wait()
     pair.wait_recv()
-    own_part = velocity_ref[0, row_slice(own)]
-    other_part = sibling_part[...]
+    here = own_part[...]
+    there = sibling_part[...]
     for d in range(DEPTH):
-        held = jnp.where(owner_ref[d] == s, own_part, jnp.zeros_like(own_part))
-        mine[d] = jnp.where(owner_ref[d] == z * 2 + 1 - c, other_part, held)
+        held = jnp.where(owner_ref[d] == s, here, jnp.zeros_like(here))
+        mine[d] = jnp.where(owner_ref[d] == z * 2 + 1 - c, there, held)
 
     def at(k):
         return pl.ds(pl.multiple_of(k * CHUNK, CHUNK), CHUNK)
@@ -281,8 +295,36 @@
     lower = z < chain // 2
     upper = z >= chain // 2
 
-    def out_copy(k):
-        return pltpu.make_async_copy(slabs.at[:, :, :, at(k)], out_ref.at[:, :, :, at(k)], out_sem.at[k])
+    def out_copy(i, k):
+        held = fields if i < 2 else stage
+        return pltpu.make_async_copy(
+            held.at[i % 2, :, :, :, at(k)], out_refs[i].at[:, 0, :, :, at(k)], out_sem.at[i, k]
+        )
+
+    def compute(k):
+        for i in range(count):
+            scale = freq_ref[i] * (0.5 / math.pi)
+            cosine, sine = cos_sin(slabs[0, :, :, at(k)].reshape(height, CHUNK) * scale)
+            sre, sim, rre, rim = [
+                fields[field, i, part, :, at(k)].astype(F32) for field in range(2) for part in range(2)
+            ]
+            re = jnp.concatenate([sre * cosine - sim * sine, rre * cosine + rim * sine], axis=1)
+            im = jnp.concatenate([sre * sine + sim * cosine, rre * sine - rim * cosine], axis=1)
+            re, im = sweep_y(*sweep_x(re.astype(BF16), im.astype(BF16), mx[i]), my[i])
+            re, im = re.astype(BF16), im.astype(BF16)
+            for field in range(2):
+                fields[field, i, 0, :, at(k)] = re[:, field * CHUNK : (field + 1) * CHUNK]
+                fields[field, i, 1, :, at(k)] = im[:, field * CHUNK : (field + 1) * CHUNK]
+            cosine, sine = cos_sin(slabs[1, :, :, at(k)].reshape(height, CHUNK) * scale)
+            cosine = jnp.concatenate([cosine, cosine], axis=1)
+            sine = jnp.concatenate([sine, sine], axis=1)
+            re, im = re.astype(F32), im.astype(F32)
+            re, im = sweep_x(
+                (re * cosine - im * sine).astype(BF16), (re * sine + im * cosine).astype(BF16), mx[i]
+            )
+            for field in range(2):
+                stage[field, i, 0, :, at(k)] = re[:, field * CHUNK : (field + 1) * CHUNK]
+                stage[field, i, 1, :, at(k)] = im[:, field * CHUNK : (field + 1) * CHUNK]
 
     def step(i, carry):
         @pl.when(i < chunks)
@@ -312,23 +354,30 @@
                 plane_copy(j, k).start()
             core_copy(0, k).start()
 
-        @pl.when(jnp.logical_and(i >= LAG + 1, i < chunks + LAG + 1))
-        def _():
-            k = i - LAG - 1
+        @pl.when(jnp.logical_and(i >= PLANE_LAG, i < chunks + PLANE_LAG))
+        def _():
+            k = i - PLANE_LAG
             for j in range(1, freqs):
                 arrived(j, k).wait_recv()
                 core_copy(j, k).start()
 
-        @pl.when(i >= LAG + 2)
-        def _():
-            k = i - LAG - 2
+        @pl.when(i == CORE_LAG)
+        def _():
+            for load in loads:
+                load.wait()
+
+        @pl.when(i >= CORE_LAG)
+        def _():
+            k = i - CORE_LAG
             for j in range(freqs):
                 core_arrived(j, k).wait_recv()
-            out_copy(k).start()
+            compute(k)
+            for out in range(4):
+                out_copy(out, k).start()
 
         return carry
 
-    lax.fori_loop(0, chunks + LAG + 2, step, 0)
+    lax.fori_loop(0, chunks + CORE_LAG, step, 0)
     pair.wait_send()
 
     def drain(k, carry):
@@ -344,37 +393,45 @@
             plane_copy(j, k).wait_send()
         for j in range(freqs):
             core_copy(j, k).wait_send()
-        out_copy(k).wait()
+        for out in range(4):
+            out_copy(out, k).wait()
         return carry
 
     lax.fori_loop(0, chunks, drain, 0)
 
 
-def exchange_slabs(freqs, shots, owners, velocity):
+def exchange_slabs(freqs, shots, owners, freq, velocity, source, receiver, xc, yc):
     _, height, width = velocity.shape
+    count = source.shape[0]
     rows = height // (2 * freqs)
     chunks = width // CHUNK
+    vmem = pl.BlockSpec(memory_space=pltpu.VMEM)
+    smem = pl.BlockSpec(memory_space=pltpu.SMEM)
+    anywhere = pl.BlockSpec(memory_space=pl.ANY)
     strip = pltpu.VMEM((DEPTH, rows, width), F32)
+    field = pltpu.VMEM((2, count, 2, height, width), BF16)
+    matrix = pltpu.VMEM((count, 256, 256), BF16)
     dma = pltpu.SemaphoreType.DMA
-    slabs = pl.pallas_call(
+    shape = jax.ShapeDtypeStruct(source.shape, BF16)
+    return pl.pallas_call(
         functools.partial(slab_kernel, freqs, shots),
-        in_specs=[pl.BlockSpec(memory_space=pltpu.SMEM), pl.BlockSpec(memory_space=pltpu.VMEM)],
-        out_specs=pl.BlockSpec(memory_space=pl.ANY),
-        out_shape=jax.ShapeDtypeStruct((DEPTH, 2 * freqs, rows, width), F32),
+        in_specs=[smem, smem, anywhere, anywhere, anywhere, vmem, vmem],
+        out_specs=[anywhere] * 4,
+        out_shape=[shape] * 4,
         scratch_shapes=[
             pltpu.VMEM((DEPTH, 2 * freqs, rows, width), F32),
             pltpu.VMEM((rows, width), F32),
-            strip, strip, strip, strip, strip,
+            pltpu.VMEM((rows, width), F32),
+            strip, strip, strip, strip, strip, field, field, matrix, matrix,
             dma((2,)), dma((2, chunks)), dma((2, chunks)),
             dma((freqs - 1, chunks)), dma((freqs - 1, chunks)),
-            dma((freqs, chunks)), dma((freqs, chunks)), dma((chunks,)),
+            dma((freqs, chunks)), dma((freqs, chunks)), dma((3,)), dma((4, chunks)),
         ],
         compiler_params=pltpu.CompilerParams(
-            collective_id=0, has_side_effects=True, vmem_limit_bytes=48 * 2**20
+            collective_id=0, has_side_effects=True, vmem_limit_bytes=56 * 2**20
         ),
-        name="exchange_slabs",
-    )(owners, velocity)
-    return slabs.reshape(DEPTH, height, width)
+        name="slabs_and_sweeps",
+    )(owners, freq, velocity, source, receiver, xc, yc)
 
 
 def image_kernel(
@@ -477,10 +534,13 @@
     velocity, slab_owner, apertures, tile_order,
 ):
     tile_ids = apertures[0]
-    slabs = exchange_slabs(freqs, shots, slab_owner, velocity)
-    source, receiver, terms = compute(
+    first_source, first_receiver, source, receiver = exchange_slabs(
+        freqs, shots, slab_owner, angular_freq, velocity, source_field, receiver_field,
+        x_correction, y_correction,
+    )
+    source, receiver, terms = last_sweep(
         angular_freq.shape[0] * freqs, tile_order.shape[0],
-        source_field, receiver_field, angular_freq, x_correction, y_correction, slabs, tile_ids,
+        tile_ids, y_correction, first_source, first_receiver, source, receiver,
     )
     return source, receiver, exchange_image(freqs, shots, tile_ids, tile_order, terms)
 

time: 108 us -> 148 us (1.37)
  Pallas kernels: 104 us -> 144 us
    pallas_call x2, Pallas kernels: 87.6 us -> 129 us  [the longest x1 120 us: exchange_slabs(): pl.pallas_call(functools.partial(slab_kernel, freqs, shots), in_specs=[sm...]
    unnamed x10 -> x8, local copies, waits for them, and re-layouts: 3.19 us -> 2.19 us
where the time goes in v3:
time: 148 us
  Pallas kernels  144 us (97%)
  local copies, waits for them, and re-layouts  2.92 us (2%)
    pallas_call x1, Pallas kernels, exchange_slabs(): pl.pallas_call(functools.partial(slab_kernel, freqs, shots), in_specs=[sm...  120 us
    pallas_call x1, Pallas kernels, exchange_image(): pl.pallas_call(functools.partial(image_kernel, freqs, shots), in_specs=[s...  14.6 us
    pallas_call x1, Pallas kernels, last_sweep(): pl.pallas_call(functools.partial(last_kernel, freq_total), grid=(width //...  9.6 us

profile of v3, /device:TPU:1, one launch (start us, length us, event | category | flops | bytes accessed | tf_op | source)
XLA Modules:
  0.0 147.6 jit_solution(5366818013034312543)
XLA Ops:
  0.6 0.0 copy-start.1
  0.6 0.0 copy-start.2
  0.7 119.7 %slabs_and_sweeps.1 = (bf16[2,1,2,128,4096]{4,3,2,1,0:T(8,128)(2,1)}, bf16[2,1,2,128,4096]{4,3,2,1,0:T(8,128)(2,1)}, bf16[2,1,2,128,4096]{4,3,2,1,0:T(8,128)(2,1)}, bf16[2,1,2,128,4096]{4,3,2,1,0:T(8,128)(2,1)}) custom-call(s32[2]{0:T(128)} %owner_ref.1, f32[2]{0:T(128)} %freq_ref.1, f32[1,128,4096]{2,1,0:T(8,128)} %velocity_ref.1, ...), custom_call_target="tpu_custom_call" | custom-call | tf_op jit(solution)/shard_map/slabs_and_sweeps/pallas_call | solution.py:416
  120.4 0.0 copy-done.1
  120.4 0.0 copy-done.2
  120.4 0.0 copy-start
  120.4 2.2 %copy-done = bf16[2,1,2,128,4096]{4,3,2,1,0:T(8,128)(2,1)S(1)} copy-done((bf16[2,1,2,128,4096]{4,3,2,1,0:T(8,128)(2,1)S(1)}, bf16[2,1,2,128,4096]{4,3,2,1,0:T(8,128)(2,1)}, u32[]{:S(2)}) %copy-start) | copy-done | bytes 4194328
  122.6 0.0 copy-start.3
  122.6 9.6 %last_sweep.1 = (bf16[2,1,2,128,4096]{4,3,2,1,0:T(8,128)(2,1)}, bf16[2,1,2,128,4096]{4,3,2,1,0:T(8,128)(2,1)}, f32[2,2,128,128]{3,2,1,0:T(8,128)S(1)}) custom-call(s32[2]{0:T(128)S(1)} %bitcast.3, bf16[2,2,128,128]{3,2,1,0:T(8,128)(2,1)S(1)} %copy-done.1, bf16[2,1,2,128,4096]{4,3,2,1,0:T(8,128)(2,1)S(1)} %copy-done, ...), custom_call_target="tpu_custom_call" | custom-call | tf_op jit(solution)/shard_map/last_sweep/pallas_call | solution.py:145
  132.2 0.0 copy-done.3
  132.2 14.6 %exchange_image.1 = f32[4,2,32,128]{3,2,1,0:T(8,128)S(1)} custom-call(s32[2]{0:T(128)S(1)} %bitcast.4, s32[32]{0:T(128)S(1)} %copy-done.3, f32[2,2,128,128]{3,2,1,0:T(8,128)S(1)} %get-tuple-element.16.term_ref), custom_call_target="tpu_custom_call" | custom-call | tf_op jit(solution)/shard_map/exchange_image/pallas_call | solution.py:513
  146.9 0.7 reshape.9
Async XLA Ops:
  0.6 119.8 %copy-start.1 = (bf16[2,2,128,128]{3,2,1,0:T(8,128)(2,1)S(1)}, bf16[2,2,128,128]{3,2,1,0:T(8,128)(2,1)}, u32[]{:S(2)}) copy-start(bf16[2,2,128,128]{3,2,1,0:T(8,128)(2,1)} %y_ref.3) | copy-start | bytes 393220
  0.6 119.8 %copy-start.2 = (s32[1,2]{1,0:T(1,128)S(1)}, s32[1,2]{1,0:T(1,128)}, u32[]{:S(2)}) copy-start(s32[1,2]{1,0:T(1,128)} %param.16) | copy-start | bytes 28
  120.4 2.2 %copy-start = (bf16[2,1,2,128,4096]{4,3,2,1,0:T(8,128)(2,1)S(1)}, bf16[2,1,2,128,4096]{4,3,2,1,0:T(8,128)(2,1)}, u32[]{:S(2)}) copy-start(bf16[2,1,2,128,4096]{4,3,2,1,0:T(8,128)(2,1)} %get-tuple-element.10.source_ref.half_source) | copy-start | bytes 12582916
  122.6 9.6 %copy-start.3 = (s32[32]{0:T(128)S(1)}, s32[32]{0:T(128)}, u32[]{:S(2)}) copy-start(s32[32]{0:T(128)} %order_ref.1) | copy-start | bytes 388

commit v4 on v3

--- a/solution.py
+++ b/solution.py
@@ -11,15 +11,15 @@
 DEPTH = 2
 TILE_DEV = 4
 CHUNK = 256
-LAST_CHUNK = 512
+LAST_CHUNK = 1024
 SIN = (4.44288292, -7.3082457, 3.60635441, -0.84611287, 0.10982695)
 COS = (1.4142135, -6.97885099, 5.73946116, -1.88356292, 0.31069804)
 F32 = jnp.float32
 BF16 = jnp.bfloat16
 MESH = pl.DeviceIdType.MESH
-LAG = 2
-PLANE_LAG = LAG + 3
-CORE_LAG = PLANE_LAG + 1
+HOP = 2
+PLANE = 3
+CORE = 2
 
 
 def horner(coefficients, z):
@@ -111,7 +111,7 @@
         receiver_out[f, 0, 0] = re.astype(BF16)
         receiver_out[f, 0, 1] = (-im).astype(BF16)
 
-    @pl.when(step == 1)
+    @pl.when(step == pl.num_programs(0) - 1)
     def _():
         for a in range(aper):
             for load in loads(a):
@@ -156,7 +156,7 @@
             pltpu.VMEM((aper, DEPTH, 2, count, 2, height, 128), BF16),
             pltpu.SemaphoreType.DMA((aper, DEPTH, 2)),
         ],
-        compiler_params=pltpu.CompilerParams(vmem_limit_bytes=48 * 2**20),
+        compiler_params=pltpu.CompilerParams(vmem_limit_bytes=60 * 2**20),
         name="last_sweep",
     )(ids, yc, source, receiver, first_source, first_receiver, source, receiver)
 
@@ -292,8 +292,9 @@
             down_out[:, :, at(k)] = down_in[:, :, at(k)] + mine[:, :, at(k)]
             down_copy(k).start()
 
-    lower = z < chain // 2
-    upper = z >= chain // 2
+    z_lag = HOP * (chain - 1)
+    plane_lag = z_lag + PLANE
+    core_lag = plane_lag + CORE
 
     def out_copy(i, k):
         held = fields if i < 2 else stage
@@ -327,48 +328,35 @@
                 stage[field, i, 1, :, at(k)] = im[:, field * CHUNK : (field + 1) * CHUNK]
 
     def step(i, carry):
-        @pl.when(i < chunks)
-        def _():
-            @pl.when(lower)
-            def _():
-                go_up(i)
-
-            @pl.when(upper)
-            def _():
-                go_down(i)
-
-        @pl.when(jnp.logical_and(i >= LAG, i < chunks + LAG))
-        def _():
-            k = i - LAG
-
-            @pl.when(lower)
-            def _():
-                go_down(k)
-
-            @pl.when(upper)
-            def _():
-                go_up(k)
-
+        for first, go in ((HOP * z, go_up), (HOP * (chain - 1 - z), go_down)):
+
+            @pl.when(jnp.logical_and(i >= first, i < chunks + first))
+            def _(first=first, go=go):
+                go(i - first)
+
+        @pl.when(jnp.logical_and(i >= z_lag, i < chunks + z_lag))
+        def _():
+            k = i - z_lag
             slabs[:, own, :, at(k)] = up_in[:, :, at(k)] + mine[:, :, at(k)] + down_in[:, :, at(k)]
             for j in range(1, freqs):
                 plane_copy(j, k).start()
             core_copy(0, k).start()
 
-        @pl.when(jnp.logical_and(i >= PLANE_LAG, i < chunks + PLANE_LAG))
-        def _():
-            k = i - PLANE_LAG
+        @pl.when(jnp.logical_and(i >= plane_lag, i < chunks + plane_lag))
+        def _():
+            k = i - plane_lag
             for j in range(1, freqs):
                 arrived(j, k).wait_recv()
                 core_copy(j, k).start()
 
-        @pl.when(i == CORE_LAG)
+        @pl.when(i == core_lag)
         def _():
             for load in loads:
                 load.wait()
 
-        @pl.when(i >= CORE_LAG)
-        def _():
-            k = i - CORE_LAG
+        @pl.when(i >= core_lag)
+        def _():
+            k = i - core_lag
             for j in range(freqs):
                 core_arrived(j, k).wait_recv()
             compute(k)
@@ -377,7 +365,7 @@
 
         return carry
 
-    lax.fori_loop(0, chunks + CORE_LAG, step, 0)
+    lax.fori_loop(0, chunks + core_lag, step, 0)
     pair.wait_send()
 
     def drain(k, carry):
@@ -428,7 +416,7 @@
             dma((freqs, chunks)), dma((freqs, chunks)), dma((3,)), dma((4, chunks)),
         ],
         compiler_params=pltpu.CompilerParams(
-            collective_id=0, has_side_effects=True, vmem_limit_bytes=56 * 2**20
+            collective_id=0, has_side_effects=True, vmem_limit_bytes=60 * 2**20
         ),
         name="slabs_and_sweeps",
     )(owners, freq, velocity, source, receiver, xc, yc)
@@ -522,7 +510,7 @@
             dma((chain,)), dma((chain,)),
         ],
         compiler_params=pltpu.CompilerParams(
-            collective_id=1, has_side_effects=True, vmem_limit_bytes=48 * 2**20
+            collective_id=1, has_side_effects=True, vmem_limit_bytes=60 * 2**20
         ),
         name="exchange_image",
     )(ids, order, terms)

time: 148 us -> 77.1 us (0.52)
  Pallas kernels: 144 us -> 74.6 us
    pallas_call x1, Pallas kernels: 120 us -> 48.7 us  [exchange_slabs(): pl.pallas_call(functools.partial(slab_kernel, freqs, shots), in_specs=[sm...]
    pallas_call x1, Pallas kernels: 14.6 us -> 16.8 us  [exchange_image(): pl.pallas_call(functools.partial(image_kernel, freqs, shots), in_specs=[s...]
    unnamed x8 -> x0, local copies, waits for them, and re-layouts: 2.19 us -> none
where the time goes in v4:
time: 77.1 us; the launch traced here: 76.9 us
  Pallas kernels  74.6 us (97%)
  local copies, waits for them, and re-layouts  1.63 us (2%)
    pallas_call x1, Pallas kernels, exchange_slabs(): pl.pallas_call(functools.partial(slab_kernel, freqs, shots), in_specs=[sm...  48.7 us
    pallas_call x1, Pallas kernels, exchange_image(): pl.pallas_call(functools.partial(image_kernel, freqs, shots), in_specs=[s...  16.8 us
    pallas_call x1, Pallas kernels, last_sweep(): pl.pallas_call(functools.partial(last_kernel, freq_total), grid=(width //...  9.1 us
    reshape x1, local copies, waits for them, and re-layouts, exchange_image(): return image.reshape(TILE_DEV, DEPTH, rows * tile_width)  1.63 us

profile of v4, /device:TPU:1, one launch (start us, length us, event | category | flops | bytes accessed | tf_op | source)
XLA Modules:
  0.0 76.9 jit_solution(14799070421804508523)
XLA Ops:
  0.6 48.7 %slabs_and_sweeps.1 = (bf16[2,1,2,128,4096]{4,3,2,1,0:T(8,128)(2,1)}, bf16[2,1,2,128,4096]{4,3,2,1,0:T(8,128)(2,1)}, bf16[2,1,2,128,4096]{4,3,2,1,0:T(8,128)(2,1)}, bf16[2,1,2,128,4096]{4,3,2,1,0:T(8,128)(2,1)}) custom-call(s32[2]{0:T(128)} %owner_ref.1, f32[2]{0:T(128)} %freq_ref.1, f32[1,128,4096]{2,1,0:T(8,128)} %velocity_ref.1, ...), custom_call_target="tpu_custom_call" | custom-call | tf_op jit(solution)/shard_map/slabs_and_sweeps/pallas_call | solution.py:404
  49.3 9.1 %last_sweep.1 = (bf16[2,1,2,128,4096]{4,3,2,1,0:T(8,128)(2,1)}, bf16[2,1,2,128,4096]{4,3,2,1,0:T(8,128)(2,1)}, f32[2,2,128,128]{3,2,1,0:T(8,128)}) custom-call(s32[2]{0:T(128)} %bitcast.3, bf16[2,2,128,128]{3,2,1,0:T(8,128)(2,1)} %y_ref.3, bf16[2,1,2,128,4096]{4,3,2,1,0:T(8,128)(2,1)} %get-tuple-element.10.source_ref.half_source, ...), custom_call_target="tpu_custom_call" | custom-call | tf_op jit(solution)/shard_map/last_sweep/pallas_call | solution.py:145
  58.4 16.8 %exchange_image.1 = f32[4,2,32,128]{3,2,1,0:T(8,128)} custom-call(s32[2]{0:T(128)} %bitcast.4, s32[32]{0:T(128)} %order_ref.1, f32[2,2,128,128]{3,2,1,0:T(8,128)} %get-tuple-element.16.term_ref), custom_call_target="tpu_custom_call" | custom-call | tf_op jit(solution)/shard_map/exchange_image/pallas_call | solution.py:501
  75.3 1.6 %reshape.9 = f32[4,2,4096]{2,1,0:T(2,128)} reshape(f32[4,2,32,128]{3,2,1,0:T(8,128)} %exchange_image.1) | data formatting | bytes 262144 | tf_op jit(solution)/shard_map/reshape | solution.py:517

commit v5 on v4

--- a/solution.py
+++ b/solution.py
@@ -10,7 +10,7 @@
 
 DEPTH = 2
 TILE_DEV = 4
-CHUNK = 256
+CHUNK = 512
 LAST_CHUNK = 1024
 SIN = (4.44288292, -7.3082457, 3.60635441, -0.84611287, 0.10982695)
 COS = (1.4142135, -6.97885099, 5.73946116, -1.88356292, 0.31069804)
@@ -18,8 +18,8 @@
 BF16 = jnp.bfloat16
 MESH = pl.DeviceIdType.MESH
 HOP = 2
-PLANE = 3
-CORE = 2
+PLANE = 2
+CORE = 1
 
 
 def horner(coefficients, z):
@@ -76,8 +76,8 @@
 
 
 def last_kernel(
-    freq_total, ids_ref, y_ref, source_ref, receiver_ref, first_source, first_receiver, half_source, half_receiver,
-    source_out, receiver_out, term_ref, my, tiles, tile_sem,
+    freq_total, ids_ref, x_ref, y_ref, source_ref, receiver_ref, first_source, first_receiver, half_source, half_receiver,
+    source_out, receiver_out, term_ref, mx, my, tiles, tile_sem,
 ):
     step = pl.program_id(0)
     aper = term_ref.shape[0]
@@ -101,13 +101,14 @@
             for load in loads(a):
                 load.start()
         for f in range(y_ref.shape[0]):
+            mx[f] = x_matrix(x_ref, f)
             my[f] = y_matrix(y_ref, f)
 
     for f in range(source_ref.shape[0]):
-        re, im = sweep_y(source_ref[f, 0, 0], source_ref[f, 0, 1], my[f])
+        re, im = sweep_y(*sweep_x(source_ref[f, 0, 0], source_ref[f, 0, 1], mx[f]), my[f])
         source_out[f, 0, 0] = re.astype(BF16)
         source_out[f, 0, 1] = im.astype(BF16)
-        re, im = sweep_y(receiver_ref[f, 0, 0], receiver_ref[f, 0, 1], my[f])
+        re, im = sweep_y(*sweep_x(receiver_ref[f, 0, 0], receiver_ref[f, 0, 1], mx[f]), my[f])
         receiver_out[f, 0, 0] = re.astype(BF16)
         receiver_out[f, 0, 1] = (-im).astype(BF16)
 
@@ -125,7 +126,7 @@
                         for part in range(2)
                     ]
                     if d == DEPTH - 1:
-                        re, im = [value.astype(BF16) for value in sweep_y(re, im, my[f])]
+                        re, im = [value.astype(BF16) for value in sweep_y(*sweep_x(re, im, mx[f]), my[f])]
                     re, im = re.astype(F32), im.astype(F32)
                     total += re[:, :128] * re[:, 128:] - im[:, :128] * im[:, 128:]
                 total = total * (1.0 / freq_total)
@@ -135,7 +136,7 @@
                 term_ref[a, d] = picked
 
 
-def last_sweep(freq_total, tile_total, ids, yc, first_source, first_receiver, source, receiver):
+def last_sweep(freq_total, tile_total, ids, xc, yc, first_source, first_receiver, source, receiver):
     count, _, _, height, width = source.shape
     aper = ids.shape[0]
     spec = pl.BlockSpec((count, 1, 2, height, LAST_CHUNK), lambda i: (0, 0, 0, 0, i))
@@ -146,19 +147,21 @@
         functools.partial(last_kernel, freq_total),
         grid=(width // LAST_CHUNK,),
         in_specs=[
-            pl.BlockSpec(memory_space=pltpu.SMEM), pl.BlockSpec(yc.shape, lambda i: (0, 0, 0, 0)),
+            pl.BlockSpec(memory_space=pltpu.SMEM),
+            pl.BlockSpec(xc.shape, lambda i: (0, 0, 0, 0)), pl.BlockSpec(yc.shape, lambda i: (0, 0, 0, 0)),
             spec, spec, anywhere, anywhere, anywhere, anywhere,
         ],
         out_specs=[spec, spec, pl.BlockSpec(term, lambda i: (0, 0, 0, 0))],
         out_shape=[shape, shape, jax.ShapeDtypeStruct(term, F32)],
         scratch_shapes=[
             pltpu.VMEM((count, 256, 256), BF16),
+            pltpu.VMEM((count, 256, 256), BF16),
             pltpu.VMEM((aper, DEPTH, 2, count, 2, height, 128), BF16),
             pltpu.SemaphoreType.DMA((aper, DEPTH, 2)),
         ],
         compiler_params=pltpu.CompilerParams(vmem_limit_bytes=60 * 2**20),
-        name="last_sweep",
-    )(ids, yc, source, receiver, first_source, first_receiver, source, receiver)
+        name="last_sweeps",
+    )(ids, xc, yc, source, receiver, first_source, first_receiver, source, receiver)
 
 
 def greet(devices, count):
@@ -320,9 +323,7 @@
             cosine = jnp.concatenate([cosine, cosine], axis=1)
             sine = jnp.concatenate([sine, sine], axis=1)
             re, im = re.astype(F32), im.astype(F32)
-            re, im = sweep_x(
-                (re * cosine - im * sine).astype(BF16), (re * sine + im * cosine).astype(BF16), mx[i]
-            )
+            re, im = (re * cosine - im * sine).astype(BF16), (re * sine + im * cosine).astype(BF16)
             for field in range(2):
                 stage[field, i, 0, :, at(k)] = re[:, field * CHUNK : (field + 1) * CHUNK]
                 stage[field, i, 1, :, at(k)] = im[:, field * CHUNK : (field + 1) * CHUNK]
@@ -528,7 +529,7 @@
     )
     source, receiver, terms = last_sweep(
         angular_freq.shape[0] * freqs, tile_order.shape[0],
-        tile_ids, y_correction, first_source, first_receiver, source, receiver,
+        tile_ids, x_correction, y_correction, first_source, first_receiver, source, receiver,
     )
     return source, receiver, exchange_image(freqs, shots, tile_ids, tile_order, terms)
 

time: 77.1 us -> 77.8 us (level)
    pallas_call x1, Pallas kernels: 9.1 us -> 11.1 us  [last_sweep(): pl.pallas_call(functools.partial(last_kernel, freq_total), grid=(width //...]
    pallas_call x1, Pallas kernels: 48.7 us -> 47.8 us  [exchange_slabs(): pl.pallas_call(functools.partial(slab_kernel, freqs, shots), in_specs=[sm...]
where the time goes in v5:
time: 77.8 us; the launch traced here: 77.6 us
  Pallas kernels  75.3 us (97%)
  local copies, waits for them, and re-layouts  1.63 us (2%)
    pallas_call x1, Pallas kernels, exchange_slabs(): pl.pallas_call(functools.partial(slab_kernel, freqs, shots), in_specs=[sm...  47.8 us
    pallas_call x1, Pallas kernels, exchange_image(): pl.pallas_call(functools.partial(image_kernel, freqs, shots), in_specs=[s...  16.4 us
    pallas_call x1, Pallas kernels, last_sweep(): pl.pallas_call(functools.partial(last_kernel, freq_total), grid=(width //...  11.1 us
    reshape x1, local copies, waits for them, and re-layouts, exchange_image(): return image.reshape(TILE_DEV, DEPTH, rows * tile_width)  1.63 us

profile of v5, /device:TPU:1, one launch (start us, length us, event | category | flops | bytes accessed | tf_op | source)
XLA Modules:
  0.0 77.6 jit_solution(5013810437022643232)
XLA Ops:
  0.6 47.8 %slabs_and_sweeps.1 = (bf16[2,1,2,128,4096]{4,3,2,1,0:T(8,128)(2,1)}, bf16[2,1,2,128,4096]{4,3,2,1,0:T(8,128)(2,1)}, bf16[2,1,2,128,4096]{4,3,2,1,0:T(8,128)(2,1)}, bf16[2,1,2,128,4096]{4,3,2,1,0:T(8,128)(2,1)}) custom-call(s32[2]{0:T(128)} %owner_ref.1, f32[2]{0:T(128)} %freq_ref.1, f32[1,128,4096]{2,1,0:T(8,128)} %velocity_ref.1, ...), custom_call_target="tpu_custom_call" | custom-call | tf_op jit(solution)/shard_map/slabs_and_sweeps/pallas_call | solution.py:405
  48.4 11.1 %last_sweeps.1 = (bf16[2,1,2,128,4096]{4,3,2,1,0:T(8,128)(2,1)}, bf16[2,1,2,128,4096]{4,3,2,1,0:T(8,128)(2,1)}, f32[2,2,128,128]{3,2,1,0:T(8,128)}) custom-call(s32[2]{0:T(128)} %bitcast.3, bf16[2,2,128,128]{3,2,1,0:T(8,128)(2,1)} %x_ref.3, bf16[2,2,128,128]{3,2,1,0:T(8,128)(2,1)} %y_ref.3, ...), custom_call_target="tpu_custom_call" | custom-call | tf_op jit(solution)/shard_map/last_sweeps/pallas_call | solution.py:146
  59.5 16.4 %exchange_image.1 = f32[4,2,32,128]{3,2,1,0:T(8,128)} custom-call(s32[2]{0:T(128)} %bitcast.4, s32[32]{0:T(128)} %order_ref.1, f32[2,2,128,128]{3,2,1,0:T(8,128)} %get-tuple-element.16.term_ref), custom_call_target="tpu_custom_call" | custom-call | tf_op jit(solution)/shard_map/exchange_image/pallas_call | solution.py:502
  76.0 1.6 %reshape.9 = f32[4,2,4096]{2,1,0:T(2,128)} reshape(f32[4,2,32,128]{3,2,1,0:T(8,128)} %exchange_image.1) | data formatting | bytes 262144 | tf_op jit(solution)/shard_map/reshape | solution.py:518

commit v6 on v4

--- a/solution.py
+++ b/solution.py
@@ -12,13 +12,14 @@
 TILE_DEV = 4
 CHUNK = 256
 LAST_CHUNK = 1024
+WHOLE = 12582912.0
 SIN = (4.44288292, -7.3082457, 3.60635441, -0.84611287, 0.10982695)
 COS = (1.4142135, -6.97885099, 5.73946116, -1.88356292, 0.31069804)
 F32 = jnp.float32
 BF16 = jnp.bfloat16
 MESH = pl.DeviceIdType.MESH
 HOP = 2
-PLANE = 3
+PLANE = 2
 CORE = 2
 
 
@@ -30,7 +31,7 @@
 
 
 def cos_sin(turns):
-    r = turns - jnp.round(turns)
+    r = turns - ((turns + WHOLE) - WHOLE)
     z = r * r
     half_sin = r * horner(SIN, z)
     half_cos = horner(COS, z)
@@ -111,7 +112,7 @@
         receiver_out[f, 0, 0] = re.astype(BF16)
         receiver_out[f, 0, 1] = (-im).astype(BF16)
 
-    @pl.when(step == pl.num_programs(0) - 1)
+    @pl.when(step == 1)
     def _():
         for a in range(aper):
             for load in loads(a):

time: 77.1 us -> 77.9 us (1.010)
  Pallas kernels: 74.6 us -> 75.4 us
    pallas_call x1, Pallas kernels: 48.7 us -> 51.4 us  [exchange_slabs(): pl.pallas_call(functools.partial(slab_kernel, freqs, shots), in_specs=[sm...]
    pallas_call x1, Pallas kernels: 16.8 us -> 15.6 us  [exchange_image(): pl.pallas_call(functools.partial(image_kernel, freqs, shots), in_specs=[s...]
where the time goes in v6:
time: 77.9 us; the launch traced here: 77.7 us
  Pallas kernels  75.4 us (97%)
  local copies, waits for them, and re-layouts  1.63 us (2%)
    pallas_call x1, Pallas kernels, exchange_slabs(): pl.pallas_call(functools.partial(slab_kernel, freqs, shots), in_specs=[sm...  51.4 us
    pallas_call x1, Pallas kernels, exchange_image(): pl.pallas_call(functools.partial(image_kernel, freqs, shots), in_specs=[s...  15.6 us
    pallas_call x1, Pallas kernels, last_sweep(): pl.pallas_call(functools.partial(last_kernel, freq_total), grid=(width //...  8.42 us
    reshape x1, local copies, waits for them, and re-layouts, exchange_image(): return image.reshape(TILE_DEV, DEPTH, rows * tile_width)  1.63 us

profile of v6, /device:TPU:1, one launch (start us, length us, event | category | flops | bytes accessed | tf_op | source)
XLA Modules:
  0.0 77.7 jit_solution(5027224192523728460)
XLA Ops:
  0.6 51.4 %slabs_and_sweeps.1 = (bf16[2,1,2,128,4096]{4,3,2,1,0:T(8,128)(2,1)}, bf16[2,1,2,128,4096]{4,3,2,1,0:T(8,128)(2,1)}, bf16[2,1,2,128,4096]{4,3,2,1,0:T(8,128)(2,1)}, bf16[2,1,2,128,4096]{4,3,2,1,0:T(8,128)(2,1)}) custom-call(s32[2]{0:T(128)} %owner_ref.1, f32[2]{0:T(128)} %freq_ref.1, f32[1,128,4096]{2,1,0:T(8,128)} %velocity_ref.1, ...), custom_call_target="tpu_custom_call" | custom-call | tf_op jit(solution)/shard_map/slabs_and_sweeps/pallas_call | solution.py:405
  52.0 8.4 %last_sweep.1 = (bf16[2,1,2,128,4096]{4,3,2,1,0:T(8,128)(2,1)}, bf16[2,1,2,128,4096]{4,3,2,1,0:T(8,128)(2,1)}, f32[2,2,128,128]{3,2,1,0:T(8,128)}) custom-call(s32[2]{0:T(128)} %bitcast.3, bf16[2,2,128,128]{3,2,1,0:T(8,128)(2,1)} %y_ref.3, bf16[2,1,2,128,4096]{4,3,2,1,0:T(8,128)(2,1)} %get-tuple-element.10.source_ref.half_source, ...), custom_call_target="tpu_custom_call" | custom-call | tf_op jit(solution)/shard_map/last_sweep/pallas_call | solution.py:146
  60.5 15.6 %exchange_image.1 = f32[4,2,32,128]{3,2,1,0:T(8,128)} custom-call(s32[2]{0:T(128)} %bitcast.4, s32[32]{0:T(128)} %order_ref.1, f32[2,2,128,128]{3,2,1,0:T(8,128)} %get-tuple-element.16.term_ref), custom_call_target="tpu_custom_call" | custom-call | tf_op jit(solution)/shard_map/exchange_image/pallas_call | solution.py:502
  76.1 1.6 %reshape.9 = f32[4,2,4096]{2,1,0:T(2,128)} reshape(f32[4,2,32,128]{3,2,1,0:T(8,128)} %exchange_image.1) | data formatting | bytes 262144 | tf_op jit(solution)/shard_map/reshape | solution.py:518
